TPU v7x, 32 devices: a whole 2x2x4 slice. The times are simulated.
32 devices in a mesh: band: 8 (over y, x, core), grid: 4 (over z).
Axes of the slice: x: 2, y: 2, z: 4, core: 2. Of those that a mesh axis runs over, the one named last changes fastest.
Arguments:
- orbitals: bfloat16 [16, 160, 25600], P('band', 'grid'), may hold values from -6 to 6
- source_index: int32 [2], replicated, may hold values from 0 to 15
Outputs:
- fock_exchange: bfloat16 [16, 160, 25600], P('band', 'grid')
All inputs are finite; a program needn't handle non-finite values.
Results may differ from a plain program's by a relative error of at most 0.012.
The roundings to bfloat16 on the way count: a program that leaves them out, or rounds other values in their place, can miss the bound.
Values may be sent and summed in bfloat16 or wider, within the bound.
No kernel may reach another device: no remote copies, remote signals or barrier semaphores. Data moves between devices by JAX's collectives and lax.ppermute only.
A program may use at most 128 MiB of HBM per device.

v0:
```python
import functools
import math

import jax
import jax.numpy as jnp
from jax import lax
from jax.experimental import pallas as pl
from jax.experimental.pallas import tpu as pltpu
from jax.sharding import PartitionSpec as P

spacing = 0.3
cores = 2


def cas_entries(rows, columns, extent):
    products_mod = rows[:, None] * columns[None, :] % extent
    radians = products_mod.astype(jnp.float32) * (2.0 * math.pi / extent)
    return ((jnp.cos(radians) + jnp.sin(radians)) / math.sqrt(extent)).astype(jnp.bfloat16)


def cas_table(extent):
    wavenum = jnp.arange(extent, dtype=jnp.int32)
    return cas_entries(wavenum, wavenum, extent)


def wave_square(indices, extent):
    folded = jnp.minimum(indices, extent - indices).astype(jnp.float32)
    return folded * folded


def coulomb_block(extent, columns, offset):
    square_x = wave_square(jnp.arange(extent, dtype=jnp.int32), extent)
    square_y = wave_square(offset + jnp.arange(columns, dtype=jnp.int32), extent)
    total_sq = square_x[:, None, None] + square_y[None, :, None] + square_x[None, None, :]
    strength = (extent * spacing) ** 2 / math.pi
    return jnp.where(total_sq > 0, strength / (total_sq + 1.0), 0.0)


def transform(grid_data, cas_matrix, pattern):
    return jnp.einsum(pattern, grid_data, cas_matrix, preferred_element_type=jnp.float32)


def broadcast(x, axis, root):
    mine = lax.axis_index(axis) == root
    return lax.psum(jnp.where(mine, x, jnp.zeros_like(x)), axis)


def slab_potentials(pair_rho, cas_matrix, kernel_block):
    along_z = transform(pair_rho, cas_matrix, "pxyz,kz->pxyk").astype(jnp.bfloat16)
    along_y = transform(along_z, cas_matrix, "pxyz,ky->pxkz").astype(jnp.bfloat16)
    turned = lax.all_to_all(along_y, "grid", split_axis=2, concat_axis=1, tiled=True)
    scaled = (kernel_block * transform(turned, cas_matrix, "pxyz,kx->pkyz")).astype(jnp.bfloat16)
    back_x = transform(scaled, cas_matrix, "pxyz,kx->pkyz").astype(jnp.bfloat16)
    returned = lax.all_to_all(back_x, "grid", split_axis=1, concat_axis=2, tiled=True)
    again_y = transform(returned, cas_matrix, "pxyz,ky->pxkz").astype(jnp.bfloat16)
    return transform(again_y, cas_matrix, "pxyz,kz->pxyk")


def fetch_source(orbitals, which):
    local_count = orbitals.shape[0]
    local_slab = lax.dynamic_index_in_dim(orbitals, which % local_count, 0, keepdims=False)
    return broadcast(local_slab, "band", which // local_count)


def slab_plan(orbitals, source_index):
    local_count, planes, _ = orbitals.shape
    extent = planes * lax.axis_size("grid")
    orbitals = orbitals.reshape(local_count, planes, extent, extent)
    source_count = source_index.shape[0]
    cas_matrix = cas_table(extent)
    columns = extent // lax.axis_size("grid")
    kernel_block = coulomb_block(extent, columns, lax.axis_index("grid") * columns)
    fetched = [fetch_source(orbitals, source_index[number]) for number in range(source_count)]
    stacked = jnp.stack(fetched)[:, None].astype(jnp.float32)
    pair_rho = (stacked * orbitals[None].astype(jnp.float32)).astype(jnp.bfloat16)
    pair_rho = pair_rho.reshape(source_count * local_count, planes, extent, extent)
    potential = slab_potentials(pair_rho, cas_matrix, kernel_block)
    potential = potential.reshape(source_count, local_count, planes, extent, extent)
    result = (-jnp.sum(stacked * potential, axis=0)).astype(jnp.bfloat16)
    return result.reshape(local_count, planes, extent * extent)


lanes = 128
quad = 4
ring = 4
turned_pitch = 161
plane_pitch = 41


def move(x, routes):
    slabs = lax.axis_size("grid")

    def place(column, core, z):
        return (column * cores + core) * slabs + z % slabs

    return lax.ppermute(x, ("band", "grid"), [(place(*a), place(*b)) for a, b in routes])


def everywhere():
    columns = lax.axis_size("band") // cores
    return [(c, k, z) for c in range(columns) for k in range(cores) for z in range(lax.axis_size("grid"))]


def swap_cores(x):
    return move(x, [((c, k, z), (c, 1 - k, z)) for c, k, z in everywhere()])


def to_column(x, d):
    return move(x, [((c, k, z), (c ^ d, k, z)) for c, k, z in everywhere()])


def to_height(x, to):
    return move(x, [((c, k, z), (c, k, to[z])) for c, k, z in everywhere() if z in to])


def holder(z):
    return z % ring // 2


def side(core):
    return 2 * core - 1


def near_routes():
    return [((c, holder(z), z + side(k)), (c, k, z)) for c, k, z in everywhere()]


def far_routes():
    return [((c, holder(z), z + 2), (c, k, z)) for c, k, z in everywhere() if k != holder(z)]


def back(routes):
    return [(b, a) for a, b in routes]


def stage(values, *earlier):
    return lax.optimization_barrier((values, earlier))[0]


def choose(first, refs, start):
    if len(refs) == 1:
        start(refs[0])
    else:
        pl.when(first)(lambda: start(refs[0]))
        pl.when(jnp.logical_not(first))(lambda: start(refs[1]))


def start_pieces(pieces, sems):
    for number, (refs, first, to) in enumerate(pieces):
        choose(first, refs, lambda ref, to=to, number=number: pltpu.make_async_copy(ref, to, sems.at[number]).start())


def wait_pieces(pieces, sems):
    for number, (refs, _, to) in enumerate(pieces):
        pltpu.make_async_copy(refs[0], to, sems.at[number]).wait()


def source_of(refs, flags, place):
    return refs, flags[2 + place] if place > 1 else 0


def source_pieces(groups, first, source, column):
    quarter = source.shape[1] // 4
    offsets = [(column ^ e) * quarter for e in range(4)]
    offsets.append(offsets[3] + quarter // 2)
    pieces = []
    for number, offset in enumerate(offsets):
        refs = [five[number].at[which] for five, which in groups]
        to = source.at[:, pl.ds(pl.multiple_of(offset, lanes), refs[0].shape[1])]
        pieces.append((refs, first, to))
    return pieces


def split(refs, *counts):
    taken = []
    for count in counts:
        taken.append(refs[:count])
        refs = refs[count:]
    return taken


def dot(a, b):
    return jnp.dot(a, b, preferred_element_type=jnp.float32)


def both(ref, rows):
    return jnp.concatenate([ref[0, rows, :], ref[1, rows, :]], axis=1)


def beside(values):
    return jnp.concatenate(values, axis=1)


def apart(value):
    return [value[:, n : n + 2 * lanes] for n in range(0, value.shape[1], 2 * lanes)]


def put_both(ref, rows, value):
    ref[0, rows, :] = value[:, :lanes]
    ref[1, rows, :] = value[:, lanes:]


def lane_ranges(pieces):
    ranges = []
    start = 0
    for piece in pieces:
        ranges.append((start, piece.shape[1]))
        start += piece.shape[1]
    return ranges


def pick_kernel(which, source_index, orbitals, *refs):
    outs, sems = refs[:-1], refs[-1]
    copies = []
    for n, (out, (orbital, start)) in enumerate(zip(outs, which(source_index))):
        copies.append(pltpu.make_async_copy(orbitals.at[orbital, :, pl.ds(start, out.shape[1])], out, sems.at[n]))
    for copy in copies:
        copy.start()
    for copy in copies:
        copy.wait()


def cut_kernel(source_index, orbitals, crossed, *refs):
    outs, sems = refs[:-1], refs[-1]
    local_count = orbitals.shape[0]
    band = lax.axis_index("band")
    core, column = lax.rem(band, cores), lax.div(band, cores)
    which = lax.rem(source_index[core], local_count)
    owner = lax.rem(lax.div(source_index[core], local_count), cores)
    width = outs[0].shape[1]
    pieces = []
    for d, out in enumerate(outs):
        lane = pl.ds(pl.multiple_of((column ^ d) * width, lanes), width)
        pieces.append(((orbitals.at[which, :, lane], crossed.at[:, lane]), owner == core, out))
    start_pieces(pieces, sems)
    wait_pieces(pieces, sems)


def put_kernel(choices, aliased, flags, *refs):
    (out, staged, sems, out_sems), refs = refs[-4:], refs[aliased:-4]
    count = len(refs) // choices
    places = [pl.ds(*lane) for lane in lane_ranges(refs[:count])]
    chosen = [refs[n::count] for n in range(count)]
    start_pieces([(refs, flags[1] == 1, staged.at[:, lane]) for refs, lane in zip(chosen, places)], sems)
    leave = []
    for number, lane in enumerate(places):
        piece = staged.at[:, lane]
        pltpu.make_async_copy(chosen[number][0], piece, sems.at[number]).wait()
        leave.append(pltpu.make_async_copy(piece, out.at[flags[0], :, lane], out_sems.at[number]))
        leave[-1].start()
    for copy in leave:
        copy.wait()


def transform_in(source, target, windows, cas, turned, out):
    planes, points = target.shape
    extent = cas.shape[0]
    step = 10
    block = quad * extent

    @pl.loop(0, points // block // step)
    def _(i):
        for r in range(quad):
            density = []
            for j in range(step):
                at = pl.ds(pl.multiple_of((i * step + j) * block + r * lanes, lanes), 2 * lanes)
                density.append(source[:, at].astype(jnp.float32) * target[:, at].astype(jnp.float32))
            density = jnp.concatenate(density, axis=0).astype(jnp.bfloat16)
            along_z = dot(density, windows[r])
            for j in range(step):
                y = (i * step + j) * quad + r
                put_both(turned, pl.ds(y, planes, stride=turned_pitch), along_z[j * planes : (j + 1) * planes])

    @pl.loop(0, planes // 8)
    def _(i):
        for j in range(8):
            x = i * 8 + j
            along_z = both(turned, pl.ds(x * turned_pitch, extent)).astype(jnp.bfloat16)
            put_both(out, pl.ds(x, extent, stride=plane_pitch), dot(cas[...], along_z))


def transform_x(slabs, into, outof, square):
    extent = square.shape[0]
    planes = extent // ring
    strength = (extent * spacing) ** 2 / math.pi
    rows = 16

    @pl.loop(0, extent // rows)
    def _(step):
        base = pl.multiple_of(step * rows * plane_pitch, 8)
        for i in range(rows):
            at = pl.ds(base + i * plane_pitch, planes)
            along_y = jnp.concatenate([both(slab, at) for slab in slabs], axis=0).astype(jnp.bfloat16)
            ky = step * rows + i
            folded = jnp.minimum(ky, extent - ky)
            weight = square[...] + (folded * folded).astype(jnp.float32) * (1.0 / strength)
            guess = pl.reciprocal(weight, approx=True)
            factor = guess * (2.0 - weight * guess)
            factor = jnp.where(weight > 1.25 / strength, factor, 0.0)
            scaled = (factor * dot(into[...], along_y)).astype(jnp.bfloat16)
            back_x = dot(outof[...], scaled)
            for n, slab in enumerate(slabs):
                put_both(slab, at, back_x[n * planes : (n + 1) * planes])


def transform_out(back_x, source, windows, cas, turned, outs):
    planes, points = source.shape
    extent = cas.shape[0]

    @pl.loop(0, planes // 8)
    def _(i):
        for j in range(8):
            x = i * 8 + j
            column_x = both(back_x, pl.ds(x, extent, stride=plane_pitch)).astype(jnp.bfloat16)
            put_both(turned, pl.ds(x * turned_pitch, extent), dot(cas[...], column_x))

    block = quad * extent
    begin = 0
    for out in outs:
        blocks = out.shape[1] // block
        step = 5 if blocks % 5 == 0 else 4

        @pl.loop(0, blocks // step)
        def _(i, begin=begin, step=step, out=out):
            first = begin + i * step
            windowed = []
            for r in range(quad):
                again_y = jnp.concatenate(
                    [both(turned, pl.ds((first + j) * quad + r, planes, stride=turned_pitch)) for j in range(step)],
                    axis=0,
                ).astype(jnp.bfloat16)
                windowed.append(dot(again_y, windows[r]))
            for j in range(step):
                w = [part[j * planes : (j + 1) * planes] for part in windowed]
                potential = [w[0][:, :lanes]]
                potential += [w[r][:, lanes:] + w[r + 1][:, :lanes] for r in range(quad - 1)]
                potential = jnp.concatenate(potential + [w[-1][:, lanes:]], axis=1)
                at = pl.ds(pl.multiple_of((first + j) * block, lanes), block)
                to = pl.ds(pl.multiple_of((i * step + j) * block, lanes), block)
                out[:, to] = (-(source[:, at].astype(jnp.float32) * potential)).astype(jnp.bfloat16)

        begin += blocks


def forward_kernel(place, first, choices, count, flags, *refs):
    targets, five, (cas, windows, _, _, out, target, source, turned, sems) = split(refs, choices * count, 5, 9)
    ranges = lane_ranges(targets[:count])
    pieces = [(targets[n::count], flags[first] == 1, target.at[:, pl.ds(*lane)]) for n, lane in enumerate(ranges)]
    pieces += source_pieces([source_of(five, flags, place)], None, source, flags[1])
    start_pieces(pieces, sems)
    wait_pieces(pieces, sems)
    transform_in(source, target, windows, cas, turned, out)


def backward_kernel(places, first, parts, flags, *refs):
    slabs, groups, (cas, windows), outs, (back_x, source, turned, sems) = split(
        refs, len(places), 5 * len(places), 2, parts, 4
    )
    chosen = [source_of(five, flags, place) for five, place in zip(split(groups, *[5] * len(places)), places)]
    pieces = [(slabs, flags[first] == 1, back_x)] + source_pieces(chosen, flags[first] == 1, source, flags[1])
    start_pieces(pieces, sems)
    wait_pieces(pieces, sems)
    transform_out(back_x, source, windows, cas, turned, outs)


def central_kernel(home, direct, flags, *refs):
    ready, targets, neighbour_source, across_source, tables, outs, scratch = split(
        refs, 3, len(refs) - 34, 5, 5, 6, 6, 9
    )
    cas, windows, windows_back, into, outof, square = tables
    given, kept, (own_out, far_out) = split(outs, 2, 2, 2)
    slabs, target, source, given_source, kept_source, turned, first_sems, later_sems, out_sems = scratch
    at_direct = flags[direct] == 1
    column = flags[1]

    count = len(targets) // 2
    ranges = lane_ranges(targets[:count])
    first = [(targets[n::count], flags[home] == 1, target.at[:, pl.ds(*lane)]) for n, lane in enumerate(ranges)]
    first += source_pieces([source_of(across_source, flags, 2)], None, source, column)
    start_pieces(first, first_sems)
    later = [((ref,), None, slabs.at[place]) for ref, place in zip(ready, (0, 1, 3))]
    near_sources = [source_of(across_source, flags, 3), source_of(neighbour_source, flags, 1)]
    later += source_pieces(near_sources, at_direct, given_source, column)
    later += source_pieces(near_sources[::-1], at_direct, kept_source, column)
    start_pieces(later, later_sems)
    wait_pieces(first, first_sems)
    transform_in(source, target, windows, cas, turned, slabs.at[2])
    wait_pieces(later, later_sems)

    transform_x([slabs.at[place] for place in range(4)], into, outof, square)

    leave = [((slabs.at[2],), None, far_out), ((slabs.at[0],), None, own_out)]
    start_pieces(leave, out_sems)
    kept_place = jnp.where(at_direct, 1, 3)
    transform_out(slabs.at[4 - kept_place], given_source, windows_back, cas, turned, given)
    transform_out(slabs.at[kept_place], kept_source, windows_back, cas, turned, kept)
    wait_pieces(leave, out_sems)


def window_tables(cas_matrix):
    extent = cas_matrix.shape[0]
    tables = []
    for r in range(quad):
        shift = r * extent % lanes
        tables.append(jnp.pad(cas_matrix, ((shift, 2 * lanes - extent - shift), (0, 2 * lanes - extent))))
    return jnp.stack(tables)


limit = 60 * 2**20
full = 64 * 2**20
whole = pl.BlockSpec(memory_space=pltpu.VMEM)
outside = pl.BlockSpec(memory_space=pl.ANY)
scalars = pl.BlockSpec(memory_space=pltpu.SMEM)
small = pl.CostEstimate(flops=10**6, bytes_accessed=10**4, transcendentals=0)


def pick(orbitals, source_index, which, widths):
    planes = orbitals.shape[1]
    return pl.pallas_call(
        functools.partial(pick_kernel, which),
        out_shape=[jax.ShapeDtypeStruct((planes, width), orbitals.dtype) for width in widths],
        in_specs=[scalars, outside],
        out_specs=[whole] * len(widths),
        scratch_shapes=[pltpu.SemaphoreType.DMA((len(widths),))],
        compiler_params=pltpu.CompilerParams(vmem_limit_bytes=limit),
        cost_estimate=small,
        name="pick",
    )(source_index, orbitals)


def cut_quarters(source_index, orbitals, crossed):
    planes, points = crossed.shape
    return pl.pallas_call(
        cut_kernel,
        out_shape=[jax.ShapeDtypeStruct((planes, points // 4), crossed.dtype)] * 4,
        in_specs=[scalars, outside, outside],
        out_specs=[whole] * 4,
        scratch_shapes=[pltpu.SemaphoreType.DMA((4,))],
        compiler_params=pltpu.CompilerParams(vmem_limit_bytes=full),
        cost_estimate=small,
        name="cut",
    )(source_index, orbitals, crossed)


def put(which, first, choices, result=None):
    pieces = [piece for choice in choices for piece in choice]
    count = len(choices[0])
    planes, points = pieces[0].shape[0], sum(piece.shape[1] for piece in choices[0])
    before = [] if result is None else [result]
    return pl.pallas_call(
        functools.partial(put_kernel, len(choices), len(before)),
        out_shape=jax.ShapeDtypeStruct((2, planes, points), pieces[0].dtype),
        in_specs=[scalars] + [outside] * (len(before) + len(pieces)),
        out_specs=outside,
        scratch_shapes=[
            pltpu.VMEM((planes, points), pieces[0].dtype),
            pltpu.SemaphoreType.DMA((count,)),
            pltpu.SemaphoreType.DMA((count,)),
        ],
        input_output_aliases={1: 0} if before else {},
        compiler_params=pltpu.CompilerParams(vmem_limit_bytes=full),
        cost_estimate=small,
        name="put",
    )(jnp.stack([which, first.astype(which.dtype)]).astype(jnp.int32), *before, *pieces)


def forward(flags, place, first, targets, group, tables):
    planes = group[0].shape[1]
    extent = tables[0].shape[0]
    points = extent * extent
    return pl.pallas_call(
        functools.partial(forward_kernel, place, first, len(targets), len(targets[0])),
        out_shape=jax.ShapeDtypeStruct((2, extent * plane_pitch, lanes), jnp.float32),
        in_specs=[scalars] + [outside] * (len(targets) * len(targets[0]) + len(group)) + [whole] * len(tables),
        out_specs=whole,
        scratch_shapes=[
            pltpu.VMEM((planes, points), jnp.bfloat16),
            pltpu.VMEM((planes, points), jnp.bfloat16),
            pltpu.VMEM((2, planes * turned_pitch, lanes), jnp.float32),
            pltpu.SemaphoreType.DMA((len(targets[0]) + 5,)),
        ],
        compiler_params=pltpu.CompilerParams(vmem_limit_bytes=limit),
        cost_estimate=small,
        name="forward",
    )(flags, *[piece for choice in targets for piece in choice], *group, *tables)


def central(flags, home, direct, ready, targets, neighbour_source, across_source, tables):
    planes = across_source[0].shape[1]
    extent = tables[0].shape[0]
    points = extent * extent
    pieces = [*ready, *targets[0], *targets[1], *neighbour_source, *across_source]
    parts = [jax.ShapeDtypeStruct((planes, share * points // 5), jnp.bfloat16) for share in (2, 3)]
    slab = jax.ShapeDtypeStruct(ready[0].shape, jnp.float32)
    outs = pl.pallas_call(
        functools.partial(central_kernel, home, direct),
        out_shape=parts * 2 + [slab] * 2,
        in_specs=[scalars] + [outside] * len(pieces) + [whole] * len(tables),
        out_specs=[whole] * 4 + [outside] * 2,
        scratch_shapes=[
            pltpu.VMEM((ring, *slab.shape), jnp.float32),
            *[pltpu.VMEM((planes, points), jnp.bfloat16)] * 4,
            pltpu.VMEM((2, planes * turned_pitch, lanes), jnp.float32),
            pltpu.SemaphoreType.DMA((len(targets[0]) + 5,)),
            pltpu.SemaphoreType.DMA((13,)),
            pltpu.SemaphoreType.DMA((2,)),
        ],
        compiler_params=pltpu.CompilerParams(vmem_limit_bytes=full),
        cost_estimate=small,
        name="central",
    )(flags, *pieces, *tables)
    return split(outs, 2, 2, 2)


def backward(flags, places, first, slabs, groups, cas_matrix, windows, parts):
    planes = groups[0][0].shape[1]
    extent = cas_matrix.shape[0]
    points = extent * extent
    pieces = [piece for group in groups for piece in group]
    return pl.pallas_call(
        functools.partial(backward_kernel, places, first, parts),
        out_shape=[jax.ShapeDtypeStruct((planes, points // parts), jnp.bfloat16)] * parts,
        in_specs=[scalars] + [outside] * (len(slabs) + len(pieces)) + [whole] * 2,
        out_specs=[whole] * parts,
        scratch_shapes=[
            pltpu.VMEM(slabs[0].shape, jnp.float32),
            pltpu.VMEM((planes, points), jnp.bfloat16),
            pltpu.VMEM((2, planes * turned_pitch, lanes), jnp.float32),
            pltpu.SemaphoreType.DMA((6,)),
        ],
        compiler_params=pltpu.CompilerParams(vmem_limit_bytes=limit),
        cost_estimate=small,
        name="backward",
    )(flags, *slabs, *pieces, cas_matrix, windows)


def add(a, b):
    return (a.astype(jnp.float32) + b.astype(jnp.float32)).astype(jnp.bfloat16)


def pair_plan(orbitals, source_index):
    local_count, planes, points = orbitals.shape
    slabs = lax.axis_size("grid")
    extent = planes * slabs
    band, z = lax.axis_index("band"), lax.axis_index("grid")
    column, core = band // cores, band % cores
    quarter = points // 4
    at_home = core == holder(z)
    direct_neighbour = core == 1 - z % 2
    parity = z % 2
    inner = (z == 1) | (z == 2)
    second = inner.astype(jnp.int32)
    flags = jnp.stack([core, column, at_home, direct_neighbour, second, 1 - second]).astype(jnp.int32)
    home, direct = 2, 3

    unit = points // 8

    def first_pieces(source_index):
        core = lax.rem(lax.axis_index("band"), cores)
        near_parity = lax.rem(lax.axis_index("grid") + 1, 2)
        candidate = lax.rem(source_index[1 - core], local_count)
        return [(candidate, 0)] + [(near_parity, start) for start in (0, unit, 6 * unit)]

    def own_orbital(source_index):
        return [(lax.rem(lax.axis_index("grid"), 2), 0)]

    other, *to_near = pick(orbitals, source_index, first_pieces, (points, unit, 5 * unit, 2 * unit))
    crossed = swap_cores(other)
    near = [move(to_near[0], near_routes())]
    owner = source_index[core] // local_count

    cuts, to_near = stage((cut_quarters(source_index, orbitals, crossed), to_near), near)
    near.append(move(to_near[1], near_routes()))
    candidates = [cuts[0]] + [to_column(cuts[d], d) for d in (1, 2, 3)]
    (own_parity,) = pick(stage(orbitals, cuts), source_index, own_orbital, (points,))
    cas_matrix = cas_table(extent)
    windows = window_tables(cas_matrix)
    windows_back = jnp.swapaxes(windows, 1, 2)
    places = (((z ^ jnp.arange(slabs)) * planes)[:, None] + jnp.arange(planes)).reshape(extent)
    into = cas_entries(jnp.arange(extent), places, extent)
    square_x = wave_square(jnp.arange(extent, dtype=jnp.int32), extent)
    strength = (extent * spacing) ** 2 / math.pi
    square = (square_x[:, None] + square_x[None, :] + 1.0) * (1.0 / strength)
    square = jnp.pad(square, ((0, 0), (0, 2 * lanes - extent)), constant_values=1.0)
    tables = [cas_matrix, windows, windows_back, into, into.T, square]

    candidates, tables, own_parity, flags = stage((candidates, tables, own_parity, flags), near)
    cas_matrix, windows, windows_back, into, outof, square = tables
    forward_tables = [cas_matrix, windows, into, outof]
    own = lax.select_n(column ^ (owner // cores), *candidates)
    own = stage(own, tables)
    own_swapped = swap_cores(own_parity)
    own_x, own_y = to_column(own, 1), to_column(own, 2)
    neighbour = to_height(own, {0: 1, 1: 0, 2: 3, 3: 2})
    crossed = to_height(own, {1: 2, 2: 1})

    neighbour, crossed, own_x, own_y, own_swapped = stage((neighbour, crossed, own_x, own_y, own_swapped))
    neighbour_x, neighbour_y = to_column(neighbour, 1), to_column(neighbour, 2)
    crossed_2 = to_height(neighbour, {1: 2, 2: 1})
    handed = to_height(crossed, {1: 0, 2: 3})

    low = jnp.stack([own_x[:, : quarter // 2], neighbour_x[:, : quarter // 2]])
    high = jnp.stack([own_y[:, quarter // 2 :], neighbour_y[:, quarter // 2 :]])
    low, high, crossed_2, own_parity, last = stage((low, high, crossed_2, own_parity, to_near[2]), handed)
    low, high = to_column(low, 2), to_column(high, 1)
    handed_2 = to_height(crossed_2, {1: 0, 2: 3})
    near.append(move(last, near_routes()))
    far = [move(own_parity, far_routes())]

    across = jnp.stack([jnp.where(inner, crossed, handed), jnp.where(inner, crossed_2, handed_2)])
    across, low, high = stage((across, low, high))
    sources = [
        [own[None], own_x[None], own_y[None], low[:1], high[:1]],
        [neighbour[None], neighbour_x[None], neighbour_y[None], low[1:], high[1:]],
    ]
    across_x, across_y = to_column(across, 1), to_column(across, 2)
    near_swapped = [swap_cores(part) for part in stage(near[:2], across)]
    along_y = [forward(flags, 0, home, [[own_parity], [own_swapped]], sources[0], forward_tables)]

    low, high = across_x[:, :, : quarter // 2], across_y[:, :, quarter // 2 :]
    near[2] = stage(near[2], along_y)
    near_swapped.append(swap_cores(near[2]))
    low, high, near_swapped = stage((low, high, near_swapped), along_y)
    low, high = to_column(low, 2), to_column(high, 1)
    along_y.append(forward(flags, 1, direct, [near, near_swapped], sources[1], forward_tables))

    low, high, far = stage((low, high, far), along_y)
    across_source = [across, across_x, across_y, low, high]
    sources += [across_source, across_source]
    far_swapped = [swap_cores(part) for part in far]
    along_y_3 = forward(flags, 3, direct, [near_swapped, near], across_source, forward_tables)
    far_swapped = stage(far_swapped, along_y_3)
    given, kept, (own_back, far_back) = central(
        flags,
        home,
        direct,
        [*along_y, along_y_3],
        [far_swapped, far],
        sources[1],
        across_source,
        [cas_matrix, windows, windows_back, into, outof, square],
    )

    def partials(places, slabs, *earlier):
        groups = [sources[place] for place in places]
        return backward(flags, places, home, stage(slabs, *earlier), groups, cas_matrix, windows_back, 4)

    near = [add(k, swap_cores(g)) for k, g in zip(kept, given)]
    near_home = [move(part, back(near_routes())) for part in near]
    given = partials([2, 0], [far_back, own_back], near[0])
    kept = partials([0, 2], [own_back, far_back], given[0], near_home[0])
    far = [add(k, swap_cores(g)) for k, g in zip(kept, given)]
    far_home = [move(part, back(far_routes())) for part in far]
    result = put(1 - parity, at_home, [near_home])
    result, far_home = stage((result, far_home))
    return put(parity, at_home, [far, far_home], result)


def solution(mesh):
    def shards(orbitals, source_index):
        slabs, bands = mesh.shape["grid"], mesh.shape["band"]
        fits = slabs == 4 and bands == 8 and orbitals.shape[0] == 2 and source_index.shape[0] == cores
        return (pair_plan if fits else slab_plan)(orbitals, source_index)

    return jax.shard_map(
        shards,
        mesh=mesh,
        in_specs=(P("band", "grid", None), P()),
        out_specs=P("band", "grid", None),
        check_vma=False,
    )
```

profile of v0, /device:TPU:1, one launch (start us, length us, event | category | flops | bytes accessed | tf_op | source)
XLA Modules:
  0.0 293.1 jit_solution(12389955542742600971)
XLA Ops:
  0.0 4.9 %pick.2 = (bf16[40,25600]{1,0:T(8,128)(2,1)}, bf16[40,3200]{1,0:T(8,128)(2,1)}, bf16[40,16000]{1,0:T(8,128)(2,1)}, bf16[40,6400]{1,0:T(8,128)(2,1)}) custom-call(s32[2]{0:T(128)} %source_index.5, bf16[2,40,25600]{2,1,0:T(8,128)(2,1)} %orbitals.4), custom_call_target="tpu_custom_call" | custom-call | flops 1000000 | bytes 10000 | tf_op jit(solution)/shard_map/pick/pallas_call | solution.py:419
  5.0 4.7 %collective-permute-start.1 = (bf16[40,3200]{1,0:T(8,128)(2,1)}, bf16[40,3200]{1,0:T(8,128)(2,1)}, u32[]{:S(2)}, u32[]{:S(2)}) collective-permute-start(bf16[40,3200]{1,0:T(8,128)(2,1)} %get-tuple-element.86), channel_id=1, source_target_pairs={{3,0},{0,1},{5,2},{6,3},{1,4},{2,5},{7,6},{4,7},{11,8},{8,9},{13,1... | collective-permute-start | bytes 768008 | tf_op jit(solution)/shard_map/ppermute | solution.py:96
  9.7 3.5 %cut.1 = (bf16[40,6400]{1,0:T(8,128)(2,1)}, bf16[40,6400]{1,0:T(8,128)(2,1)}, bf16[40,6400]{1,0:T(8,128)(2,1)}, bf16[40,6400]{1,0:T(8,128)(2,1)}) custom-call(s32[2]{0:T(128)} %source_index.5, bf16[2,40,25600]{2,1,0:T(8,128)(2,1)} %orbitals.4, bf16[40,25600]{1,0:T(8,128)(2,1)} %collective-permute-done.crossed), custom_call_target="tpu_custom_call" | custom-call | flops 1000000 | bytes 10000 | tf_op jit(solution)/shard_map/cut/pallas_call | solution.py:433
  14.5 3.7 %collective-permute-start.5 = (bf16[40,16000]{1,0:T(8,128)(2,1)}, bf16[40,16000]{1,0:T(8,128)(2,1)}, u32[]{:S(2)}, u32[]{:S(2)}) collective-permute-start(bf16[40,16000]{1,0:T(8,128)(2,1)} %get-tuple-element.94), channel_id=1, source_target_pairs={{3,0},{0,1},{5,2},{6,3},{1,4},{2,5},{7,6},{4,7},{11,8},{8,9},{13,1... | collective-permute-start | bytes 3840008 | tf_op jit(solution)/shard_map/ppermute | solution.py:96
  21.9 1.3 dynamic_slice.3
  28.2 1.5 multiply_convert_fusion
  29.8 3.7 %pick.3.refs_0_ = bf16[40,25600]{1,0:T(8,128)(2,1)} custom-call(s32[2]{0:T(128)} %source_index.5, bf16[2,40,25600]{2,1,0:T(8,128)(2,1)} %orbitals.4), custom_call_target="tpu_custom_call" | custom-call | flops 1000000 | bytes 10000 | tf_op jit(solution)/shard_map/pick/pallas_call | solution.py:419
  33.5 11.0 %collective-permute-done.3 = bf16[40,6400]{1,0:T(8,128)(2,1)S(1)} collective-permute-done((bf16[40,6400]{1,0:T(8,128)(2,1)}, bf16[40,6400]{1,0:T(8,128)(2,1)S(1)}, u32[]{:S(2)}, u32[]{:S(2)}) %collective-permute-start.3) | collective-permute-done | bytes 512032 | tf_op jit(solution)/shard_map/ppermute | solution.py:96
  45.8 1.9 collective-permute-start.10
  47.8 1.3 collective-permute-start.9
  51.1 1.3 collective-permute-start.6
  55.6 5.6 %collective-permute-done.9 = bf16[40,6400]{1,0:T(8,128)(2,1)S(1)} collective-permute-done((bf16[40,6400]{1,0:T(8,128)(2,1)S(1)}, bf16[40,6400]{1,0:T(8,128)(2,1)S(1)}, u32[]{:S(2)}, u32[]{:S(2)}) %collective-permute-start.9) | collective-permute-done | bytes 512032 | tf_op jit(solution)/shard_map/ppermute | solution.py:96
  62.1 1.6 collective-permute-done.6
  65.0 1.3 collective-permute-start.14
  66.4 9.9 %collective-permute-done.12 = bf16[40,6400]{1,0:T(8,128)(2,1)S(1)} collective-permute-done((bf16[40,6400]{1,0:T(8,128)(2,1)S(1)}, bf16[40,6400]{1,0:T(8,128)(2,1)S(1)}, u32[]{:S(2)}, u32[]{:S(2)}) %collective-permute-start.12) | collective-permute-done | bytes 512032 | tf_op jit(solution)/shard_map/ppermute | solution.py:96
  76.5 2.8 collective-permute-done.14
  81.8 1.5 collective-permute-start.18
  83.3 1.3 collective-permute-start.15
  84.6 8.8 %collective-permute-start.26 = (bf16[40,25600]{1,0:T(8,128)(2,1)}, bf16[40,25600]{1,0:T(8,128)(2,1)}, u32[]{:S(2)}, u32[]{:S(2)}) collective-permute-start(bf16[40,25600]{1,0:T(8,128)(2,1)} %pick.3.refs_0_), channel_id=1, source_target_pairs={{4,2},{5,3},{2,4},{3,5},{12,10},{13,11},{10,12},{11,13},{20,18},{2... | collective-permute-start | bytes 6144008 | tf_op jit(solution)/shard_map/ppermute | solution.py:96
  93.5 10.9 %collective-permute-done.15 = bf16[40,6400]{1,0:T(8,128)(2,1)S(1)} collective-permute-done((bf16[40,6400]{1,0:T(8,128)(2,1)S(1)}, bf16[40,6400]{1,0:T(8,128)(2,1)S(1)}, u32[]{:S(2)}, u32[]{:S(2)}) %collective-permute-start.15) | collective-permute-done | bytes 512032 | tf_op jit(solution)/shard_map/ppermute | solution.py:96
  106.5 5.1 %collective-permute-start.22 = (bf16[40,16000]{1,0:T(8,128)(2,1)}, bf16[40,16000]{1,0:T(8,128)(2,1)}, u32[]{:S(2)}, u32[]{:S(2)}) collective-permute-start(bf16[40,16000]{1,0:T(8,128)(2,1)} %collective-permute-done.5.refs_1_.refs_4_), channel_id=1, source_target_pairs={{0,4},{1,5},{2,6},{3,7},{4,0},{5,1},{6,2},{7,3},{8,12},{9,13},{10,... | collective-permute-start | bytes 3840008 | tf_op jit(solution)/shard_map/ppermute | solution.py:96
  112.4 9.2 %forward.3.refs_0_ = f32[2,6560,128]{2,1,0:T(8,128)} custom-call(s32[6]{0:T(128)} %stack.100.flags, bf16[40,25600]{1,0:T(8,128)(2,1)} %pick.3.refs_0_, bf16[40,25600]{1,0:T(8,128)(2,1)} %collective-permute-done.10.refs_1_, bf16[1,40,6400]{2,1,0:T(8,128)(2,1)} %bitcast.37, bf16[1,40,6400]{2,1,0:T(8,128)(2,1)} %bitcast.43, bf16[1,40,6400]{2,1,0:T(8,128)(2,1)} %bitcast.40, ...), custom_call_target="tpu_custom_call" | custom-call | flops 1000000 | bytes 10000 | tf_op jit(solution)/shard_map/forward/pallas_call | solution.py:471
  121.8 2.9 collective-permute-done.20.refs_8_.refs_12_.refs_4_.refs_9_
  124.6 5.1 %collective-permute-start.21 = (bf16[40,3200]{1,0:T(8,128)(2,1)}, bf16[40,3200]{1,0:T(8,128)(2,1)S(1)}, u32[]{:S(2)}, u32[]{:S(2)}) collective-permute-start(bf16[40,3200]{1,0:T(8,128)(2,1)} %collective-permute-done.1.refs_0_.refs_3_), channel_id=1, source_target_pairs={{0,4},{1,5},{2,6},{3,7},{4,0},{5,1},{6,2},{7,3},{8,12},{9,13},{10,... | collective-permute-start | bytes 768008 | tf_op jit(solution)/shard_map/ppermute | solution.py:96
  133.3 9.4 %forward.4.refs_1_ = f32[2,6560,128]{2,1,0:T(8,128)} custom-call(s32[6]{0:T(128)} %stack.100.flags, bf16[40,3200]{1,0:T(8,128)(2,1)} %collective-permute-done.1.refs_0_.refs_3_, bf16[40,16000]{1,0:T(8,128)(2,1)} %collective-permute-done.5.refs_1_.refs_4_, bf16[40,6400]{1,0:T(8,128)(2,1)} %copy-done.10, bf16[40,3200]{1,0:T(8,128)(2,1)} %copy-done.14, ...), custom_call_target="tpu_custom_call" | custom-call | flops 1000000 | bytes 10000 | tf_op jit(solution)/shard_map/forward/pallas_call | solution.py:471
  142.7 3.0 %collective-permute-done.24.refs_9_.refs_13_.refs_5_.refs_10_ = bf16[2,40,3200]{2,1,0:T(8,128)(2,1)S(1)} collective-permute-done((bf16[2,40,3200]{2,1,0:T(8,128)(2,1)}, bf16[2,40,3200]{2,1,0:T(8,128)(2,1)S(1)}, u32[]{:S(2)}, u32[]{:S(2)}) %collective-permute-start.24) | collective-permute-done | bytes 512032 | tf_op jit(solution)/shard_map/ppermute | solution.py:96
  146.7 9.3 %forward.5.refs_2_ = f32[2,6560,128]{2,1,0:T(8,128)} custom-call(s32[6]{0:T(128)} %stack.100.flags, bf16[40,3200]{1,0:T(8,128)(2,1)} %copy-done.14, bf16[40,16000]{1,0:T(8,128)(2,1)} %collective-permute-done.22.refs_4_.refs_1_, bf16[40,6400]{1,0:T(8,128)(2,1)} %copy-done.11, bf16[40,3200]{1,0:T(8,128)(2,1)} %collective-permute-done.1.refs_0_.refs_3_, ...), custom_call_target="tpu_custom_call" | custom-call | flops 1000000 | bytes 10000 | tf_op jit(solution)/shard_map/forward/pallas_call | solution.py:471
  156.1 34.9 %central.1 = (bf16[40,10240]{1,0:T(8,128)(2,1)}, bf16[40,15360]{1,0:T(8,128)(2,1)}, bf16[40,10240]{1,0:T(8,128)(2,1)}, bf16[40,15360]{1,0:T(8,128)(2,1)}, f32[2,...) custom-call(s32[6]{0:T(128)} %stack.100.flags, f32[2,6560,128]{2,1,0:T(8,128)} %forward.3.refs_0_, ...), custom_call_target="tpu_custom_call" | custom-call | flops 1000000 | bytes 10000 | tf_op jit(solution)/shard_map/central/pallas_call | solution.py:495
  191.8 2.1 collective-permute-done.28
  193.9 2.2 add_convert_fusion.1
  196.2 9.7 %backward.2 = (bf16[40,6400]{1,0:T(8,128)(2,1)}, bf16[40,6400]{1,0:T(8,128)(2,1)}, bf16[40,6400]{1,0:T(8,128)(2,1)}, bf16[40,6400]{1,0:T(8,128)(2,1)}) custom-call(s32[6]{0:T(128)} %stack.100.flags, f32[2,6560,128]{2,1,0:T(8,128)} %get-tuple-element.144.refs_0_.refs_1_, f32[2,6560,128]{2,1,0:T(8,128)} %get-tuple-element.143.refs_1_.refs_0_, ...), custom_call_target="tpu_custom_call" | custom-call | flops 1000000 | bytes 10000 | tf_op jit(solution)/shard_map/backward/pallas_call | solution.py:520
  205.9 4.1 %collective-permute-start.34 = (bf16[40,6400]{1,0:T(8,128)(2,1)}, bf16[40,6400]{1,0:T(8,128)(2,1)}, u32[]{:S(2)}, u32[]{:S(2)}) collective-permute-start(bf16[40,6400]{1,0:T(8,128)(2,1)} %get-tuple-element.147), channel_id=1, source_target_pairs={{0,4},{1,5},{2,6},{3,7},{4,0},{5,1},{6,2},{7,3},{8,12},{9,13},{10,... | collective-permute-start | bytes 1536008 | tf_op jit(solution)/shard_map/ppermute | solution.py:96
  210.9 7.0 %collective-permute-done.29.refs_0_ = bf16[40,10240]{1,0:T(8,128)(2,1)} collective-permute-done((bf16[40,10240]{1,0:T(8,128)(2,1)}, bf16[40,10240]{1,0:T(8,128)(2,1)}, u32[]{:S(2)}, u32[]{:S(2)}) %collective-permute-start.29) | collective-permute-done | bytes 819232 | tf_op jit(solution)/shard_map/ppermute | solution.py:96
  217.9 9.6 %backward.3 = (bf16[40,6400]{1,0:T(8,128)(2,1)}, bf16[40,6400]{1,0:T(8,128)(2,1)}, bf16[40,6400]{1,0:T(8,128)(2,1)}, bf16[40,6400]{1,0:T(8,128)(2,1)}) custom-call(s32[6]{0:T(128)} %stack.100.flags, f32[2,6560,128]{2,1,0:T(8,128)} %get-tuple-element.143.refs_1_.refs_0_, f32[2,6560,128]{2,1,0:T(8,128)} %get-tuple-element.144.refs_0_.refs_1_, ...), custom_call_target="tpu_custom_call" | custom-call | flops 1000000 | bytes 10000 | tf_op jit(solution)/shard_map/backward/pallas_call | solution.py:520
  227.6 2.2 add_convert_fusion.4.refs_2_
  229.7 2.3 collective-permute-start.35
  232.0 2.1 add_convert_fusion.3.refs_3_
  234.1 4.2 %collective-permute-start.37 = (bf16[40,6400]{1,0:T(8,128)(2,1)}, bf16[40,6400]{1,0:T(8,128)(2,1)}, u32[]{:S(2)}, u32[]{:S(2)}) collective-permute-start(bf16[40,6400]{1,0:T(8,128)(2,1)} %add_convert_fusion.3.refs_3_), channel_id=1, source_target_pairs={{2,4},{3,5},{4,2},{5,3},{10,12},{11,13},{12,10},{13,11},{18,20},{1... | collective-permute-start | bytes 1536008 | tf_op jit(solution)/shard_map/ppermute | solution.py:96
  238.3 2.0 add_convert_fusion.2.refs_4_
  240.3 2.3 collective-permute-start.39
  242.6 2.0 add_convert_fusion.5.refs_1_
  244.6 4.2 %collective-permute-start.33 = (bf16[40,6400]{1,0:T(8,128)(2,1)}, bf16[40,6400]{1,0:T(8,128)(2,1)}, u32[]{:S(2)}, u32[]{:S(2)}) collective-permute-start(bf16[40,6400]{1,0:T(8,128)(2,1)} %add_convert_fusion.5.refs_1_), channel_id=1, source_target_pairs={{2,4},{3,5},{4,2},{5,3},{10,12},{11,13},{12,10},{13,11},{18,20},{1... | collective-permute-start | bytes 1536008 | tf_op jit(solution)/shard_map/ppermute | solution.py:96
  249.9 3.3 %put.2.refs_0_ = bf16[2,40,25600]{2,1,0:T(8,128)(2,1)} custom-call(s32[2]{0:T(128)} %pad_add_fusion.1.flags, bf16[40,10240]{1,0:T(8,128)(2,1)} %collective-permute-done.29.refs_0_, bf16[40,15360]{1,0:T(8,128)(2,1)} %collective-permute-done.31.refs_1_), custom_call_target="tpu_custom_call" | custom-call | flops 1000000 | bytes 10000 | tf_op jit(solution)/shard_map/put/pallas_call | solution.py:450
  253.2 20.2 %collective-permute-done.35.refs_6_ = bf16[40,6400]{1,0:T(8,128)(2,1)} collective-permute-done((bf16[40,6400]{1,0:T(8,128)(2,1)}, bf16[40,6400]{1,0:T(8,128)(2,1)}, u32[]{:S(2)}, u32[]{:S(2)}) %collective-permute-start.35) | collective-permute-done | bytes 512032 | tf_op jit(solution)/shard_map/ppermute | solution.py:96
  273.4 5.5 %collective-permute-done.37.refs_7_ = bf16[40,6400]{1,0:T(8,128)(2,1)} collective-permute-done((bf16[40,6400]{1,0:T(8,128)(2,1)}, bf16[40,6400]{1,0:T(8,128)(2,1)}, u32[]{:S(2)}, u32[]{:S(2)}) %collective-permute-start.37) | collective-permute-done | bytes 512032 | tf_op jit(solution)/shard_map/ppermute | solution.py:96
  278.9 5.5 %collective-permute-done.39.refs_8_ = bf16[40,6400]{1,0:T(8,128)(2,1)} collective-permute-done((bf16[40,6400]{1,0:T(8,128)(2,1)}, bf16[40,6400]{1,0:T(8,128)(2,1)}, u32[]{:S(2)}, u32[]{:S(2)}) %collective-permute-start.39) | collective-permute-done | bytes 512032 | tf_op jit(solution)/shard_map/ppermute | solution.py:96
  284.4 5.5 %collective-permute-done.33.refs_5_ = bf16[40,6400]{1,0:T(8,128)(2,1)} collective-permute-done((bf16[40,6400]{1,0:T(8,128)(2,1)}, bf16[40,6400]{1,0:T(8,128)(2,1)}, u32[]{:S(2)}, u32[]{:S(2)}) %collective-permute-start.33) | collective-permute-done | bytes 512032 | tf_op jit(solution)/shard_map/ppermute | solution.py:96
  289.9 3.1 %put.3 = bf16[2,40,25600]{2,1,0:T(8,128)(2,1)} custom-call(s32[2]{0:T(128)} %pad_add_fusion.flags, bf16[2,40,25600]{2,1,0:T(8,128)(2,1)} %put.2.refs_0_, bf16[40,6400]{1,0:T(8,128)(2,1)} %add_convert_fusion.5.refs_1_, bf16[40,6400]{1,0:T(8,128)(2,1)} %add_convert_fusion.4.refs_2_, ...), custom_call_target="tpu_custom_call", output_to_operand_aliasing={{}: (1, {})} | custom-call | flops 1000000 | bytes 10000 | tf_op jit(solution)/shard_map/put/pallas_call | solution.py:450
  (118 shorter events, 29.3 us)
Async XLA Ops:
  4.9 4.8 %collective-permute-start = (bf16[40,25600]{1,0:T(8,128)(2,1)}, bf16[40,25600]{1,0:T(8,128)(2,1)}, u32[]{:S(2)}, u32[]{:S(2)}) collective-permute-start(bf16[40,25600]{1,0:T(8,128)(2,1)} %get-tuple-element.81), channel_id=1, source_target_pairs={{0,4},{1,5},{2,6},{3,7},{4,0},{5,1},{6,2},{7,3},{8,12},{9,13},{10,... | collective-permute-start | bytes 6144008 | tf_op jit(solution)/shard_map/ppermute | solution.py:96
  5.0 9.6 %collective-permute-start.1 = (bf16[40,3200]{1,0:T(8,128)(2,1)}, bf16[40,3200]{1,0:T(8,128)(2,1)}, u32[]{:S(2)}, u32[]{:S(2)}) collective-permute-start(bf16[40,3200]{1,0:T(8,128)(2,1)} %get-tuple-element.86), channel_id=1, source_target_pairs={{3,0},{0,1},{5,2},{6,3},{1,4},{2,5},{7,6},{4,7},{11,8},{8,9},{13,1... | collective-permute-start | bytes 768008 | tf_op jit(solution)/shard_map/ppermute | solution.py:96
  14.5 31.2 %collective-permute-start.5 = (bf16[40,16000]{1,0:T(8,128)(2,1)}, bf16[40,16000]{1,0:T(8,128)(2,1)}, u32[]{:S(2)}, u32[]{:S(2)}) collective-permute-start(bf16[40,16000]{1,0:T(8,128)(2,1)} %get-tuple-element.94), channel_id=1, source_target_pairs={{3,0},{0,1},{5,2},{6,3},{1,4},{2,5},{7,6},{4,7},{11,8},{8,9},{13,1... | collective-permute-start | bytes 3840008 | tf_op jit(solution)/shard_map/ppermute | solution.py:96
  18.4 15.1 %collective-permute-start.2 = (bf16[40,6400]{1,0:T(8,128)(2,1)}, bf16[40,6400]{1,0:T(8,128)(2,1)S(1)}, u32[]{:S(2)}, u32[]{:S(2)}) collective-permute-start(bf16[40,6400]{1,0:T(8,128)(2,1)} %get-tuple-element.90), channel_id=1, source_target_pairs={{0,8},{1,9},{2,10},{3,11},{4,12},{5,13},{6,14},{7,15},{8,0},{9,1},... | collective-permute-start | bytes 1536008 | tf_op jit(solution)/shard_map/ppermute | solution.py:96
  19.7 24.8 %collective-permute-start.3 = (bf16[40,6400]{1,0:T(8,128)(2,1)}, bf16[40,6400]{1,0:T(8,128)(2,1)S(1)}, u32[]{:S(2)}, u32[]{:S(2)}) collective-permute-start(bf16[40,6400]{1,0:T(8,128)(2,1)} %get-tuple-element.91), channel_id=1, source_target_pairs={{0,16},{1,17},{2,18},{3,19},{4,20},{5,21},{6,22},{7,23},{8,24},{9,... | collective-permute-start | bytes 1536008 | tf_op jit(solution)/shard_map/ppermute | solution.py:96
  20.9 23.6 %collective-permute-start.4 = (bf16[40,6400]{1,0:T(8,128)(2,1)}, bf16[40,6400]{1,0:T(8,128)(2,1)S(1)}, u32[]{:S(2)}, u32[]{:S(2)}) collective-permute-start(bf16[40,6400]{1,0:T(8,128)(2,1)} %get-tuple-element.92), channel_id=1, source_target_pairs={{0,24},{1,25},{2,26},{3,27},{4,28},{5,29},{6,30},{7,31},{8,16},{9,... | collective-permute-start | bytes 1536008 | tf_op jit(solution)/shard_map/ppermute | solution.py:96
  29.8 17.9 %copy-start.17 = (bf16[40,6400]{1,0:T(8,128)(2,1)S(1)}, bf16[40,6400]{1,0:T(8,128)(2,1)}, u32[]{:S(2)}) copy-start(bf16[40,6400]{1,0:T(8,128)(2,1)} %get-tuple-element.96) | copy-start | bytes 1536004
  45.8 18.0 %collective-permute-start.10 = (bf16[40,25600]{1,0:T(8,128)(2,1)}, bf16[40,25600]{1,0:T(8,128)(2,1)}, u32[]{:S(2)}, u32[]{:S(2)}) collective-permute-start(bf16[40,25600]{1,0:T(8,128)(2,1)} %pick.3.refs_0_), channel_id=1, source_target_pairs={{0,4},{1,5},{2,6},{3,7},{4,0},{5,1},{6,2},{7,3},{8,12},{9,13},{10,... | collective-permute-start | bytes 6144008 | tf_op jit(solution)/shard_map/ppermute | solution.py:96
  47.8 28.6 %copy-start.3 = (bf16[40,6400]{1,0:T(8,128)(2,1)}, bf16[40,6400]{1,0:T(8,128)(2,1)S(1)}, u32[]{:S(2)}) copy-start(bf16[40,6400]{1,0:T(8,128)(2,1)S(1)} %select_select_fusion) | copy-start | bytes 1536004
  47.8 13.4 %collective-permute-start.9 = (bf16[40,6400]{1,0:T(8,128)(2,1)S(1)}, bf16[40,6400]{1,0:T(8,128)(2,1)S(1)}, u32[]{:S(2)}, u32[]{:S(2)}) collective-permute-start(bf16[40,6400]{1,0:T(8,128)(2,1)S(1)} %select_select_fusion), channel_id=1, source_target_pairs={{0,16},{1,17},{2,18},{3,19},{4,20},{5,21},{6,22},{7,23},{8,24},{9,... | collective-permute-start | bytes 1536008 | tf_op jit(solution)/shard_map/ppermute | solution.py:96
  49.2 13.0 %collective-permute-start.8 = (bf16[40,6400]{1,0:T(8,128)(2,1)S(1)}, bf16[40,6400]{1,0:T(8,128)(2,1)S(1)}, u32[]{:S(2)}, u32[]{:S(2)}) collective-permute-start(bf16[40,6400]{1,0:T(8,128)(2,1)S(1)} %select_select_fusion), channel_id=1, source_target_pairs={{0,8},{1,9},{2,10},{3,11},{4,12},{5,13},{6,14},{7,15},{8,0},{9,1},... | collective-permute-start | bytes 1536008 | tf_op jit(solution)/shard_map/ppermute | solution.py:96
  50.4 11.8 %collective-permute-start.7 = (bf16[40,6400]{1,0:T(8,128)(2,1)S(1)}, bf16[40,6400]{1,0:T(8,128)(2,1)S(1)}, u32[]{:S(2)}, u32[]{:S(2)}) collective-permute-start(bf16[40,6400]{1,0:T(8,128)(2,1)S(1)} %select_select_fusion), channel_id=1, source_target_pairs={{1,2},{2,1},{5,6},{6,5},{9,10},{10,9},{13,14},{14,13},{17,18},{18,... | collective-permute-start | bytes 1536008 | tf_op jit(solution)/shard_map/ppermute | solution.py:96
  51.1 12.7 %collective-permute-start.6 = (bf16[40,6400]{1,0:T(8,128)(2,1)S(1)}, bf16[40,6400]{1,0:T(8,128)(2,1)S(1)}, u32[]{:S(2)}, u32[]{:S(2)}) collective-permute-start(bf16[40,6400]{1,0:T(8,128)(2,1)S(1)} %select_select_fusion), channel_id=1, source_target_pairs={{0,1},{1,0},{2,3},{3,2},{4,5},{5,4},{6,7},{7,6},{8,9},{9,8},{10,11... | collective-permute-start | bytes 1536008 | tf_op jit(solution)/shard_map/ppermute | solution.py:96
  55.6 26.2 %copy-start.18 = (bf16[40,6400]{1,0:T(8,128)(2,1)S(1)}, bf16[40,6400]{1,0:T(8,128)(2,1)}, u32[]{:S(2)}) copy-start(bf16[40,6400]{1,0:T(8,128)(2,1)} %get-tuple-element.120) | copy-start | bytes 1536004
  61.2 15.3 %copy-start.6 = (bf16[40,6400]{1,0:T(8,128)(2,1)}, bf16[40,6400]{1,0:T(8,128)(2,1)S(1)}, u32[]{:S(2)}) copy-start(bf16[40,6400]{1,0:T(8,128)(2,1)S(1)} %collective-permute-done.9) | copy-start | bytes 1536004
  63.8 15.5 %collective-permute-start.13 = (bf16[40,6400]{1,0:T(8,128)(2,1)S(1)}, bf16[40,6400]{1,0:T(8,128)(2,1)S(1)}, u32[]{:S(2)}, u32[]{:S(2)}) collective-permute-start(bf16[40,6400]{1,0:T(8,128)(2,1)S(1)} %collective-permute-done.6), channel_id=1, source_target_pairs={{1,2},{2,1},{5,6},{6,5},{9,10},{10,9},{13,14},{14,13},{17,18},{18,... | collective-permute-start | bytes 1536008 | tf_op jit(solution)/shard_map/ppermute | solution.py:96
  64.5 11.8 %collective-permute-start.12 = (bf16[40,6400]{1,0:T(8,128)(2,1)S(1)}, bf16[40,6400]{1,0:T(8,128)(2,1)S(1)}, u32[]{:S(2)}, u32[]{:S(2)}) collective-permute-start(bf16[40,6400]{1,0:T(8,128)(2,1)S(1)} %collective-permute-done.6), channel_id=1, source_target_pairs={{0,16},{1,17},{2,18},{3,19},{4,20},{5,21},{6,22},{7,23},{8,24},{9,... | collective-permute-start | bytes 1536008 | tf_op jit(solution)/shard_map/ppermute | solution.py:96
  64.8 11.5 %collective-permute-start.11 = (bf16[40,6400]{1,0:T(8,128)(2,1)S(1)}, bf16[40,6400]{1,0:T(8,128)(2,1)S(1)}, u32[]{:S(2)}, u32[]{:S(2)}) collective-permute-start(bf16[40,6400]{1,0:T(8,128)(2,1)S(1)} %collective-permute-done.6), channel_id=1, source_target_pairs={{0,8},{1,9},{2,10},{3,11},{4,12},{5,13},{6,14},{7,15},{8,0},{9,1},... | collective-permute-start | bytes 1536008 | tf_op jit(solution)/shard_map/ppermute | solution.py:96
  65.0 14.3 %collective-permute-start.14 = (bf16[40,6400]{1,0:T(8,128)(2,1)S(1)}, bf16[40,6400]{1,0:T(8,128)(2,1)S(1)}, u32[]{:S(2)}, u32[]{:S(2)}) collective-permute-start(bf16[40,6400]{1,0:T(8,128)(2,1)S(1)} %collective-permute-done.7), channel_id=1, source_target_pairs={{1,0},{2,3},{5,4},{6,7},{9,8},{10,11},{13,12},{14,15},{17,16},{18,... | collective-permute-start | bytes 1536008 | tf_op jit(solution)/shard_map/ppermute | solution.py:96
  76.3 17.2 %copy-start.8 = (bf16[40,6400]{1,0:T(8,128)(2,1)}, bf16[40,6400]{1,0:T(8,128)(2,1)S(1)}, u32[]{:S(2)}) copy-start(bf16[40,6400]{1,0:T(8,128)(2,1)S(1)} %collective-permute-done.12) | copy-start | bytes 1536004
  76.3 17.1 %copy-start.9 = (bf16[40,6400]{1,0:T(8,128)(2,1)}, bf16[40,6400]{1,0:T(8,128)(2,1)S(1)}, u32[]{:S(2)}) copy-start(bf16[40,6400]{1,0:T(8,128)(2,1)S(1)} %collective-permute-done.11) | copy-start | bytes 1536004
  79.3 25.3 %collective-permute-start.16 = (bf16[2,40,3200]{2,1,0:T(8,128)(2,1)S(1)}, bf16[2,40,3200]{2,1,0:T(8,128)(2,1)S(1)}, u32[]{:S(2)}, u32[]{:S(2)}) collective-permute-start(bf16[2,40,3200]{2,1,0:T(8,128)(2,1)S(1)} %pad_maximum_fusion.2), channel_id=1, source_target_pairs={{0,16},{1,17},{2,18},{3,19},{4,20},{5,21},{6,22},{7,23},{8,24},{9,... | collective-permute-start | bytes 1536008 | tf_op jit(solution)/shard_map/ppermute | solution.py:96
  80.5 24.1 %collective-permute-start.17 = (bf16[2,40,3200]{2,1,0:T(8,128)(2,1)S(1)}, bf16[2,40,3200]{2,1,0:T(8,128)(2,1)S(1)}, u32[]{:S(2)}, u32[]{:S(2)}) collective-permute-start(bf16[2,40,3200]{2,1,0:T(8,128)(2,1)S(1)} %pad_maximum_fusion.3), channel_id=1, source_target_pairs={{0,8},{1,9},{2,10},{3,11},{4,12},{5,13},{6,14},{7,15},{8,0},{9,1},... | collective-permute-start | bytes 1536008 | tf_op jit(solution)/shard_map/ppermute | solution.py:96
  81.8 39.9 %collective-permute-start.18 = (bf16[40,6400]{1,0:T(8,128)(2,1)S(1)}, bf16[40,6400]{1,0:T(8,128)(2,1)S(1)}, u32[]{:S(2)}, u32[]{:S(2)}) collective-permute-start(bf16[40,6400]{1,0:T(8,128)(2,1)S(1)} %copy-done.18), channel_id=1, source_target_pairs={{3,0},{0,1},{5,2},{6,3},{1,4},{2,5},{7,6},{4,7},{11,8},{8,9},{13,1... | collective-permute-start | bytes 1536008 | tf_op jit(solution)/shard_map/ppermute | solution.py:96
  83.3 21.1 %collective-permute-start.15 = (bf16[40,6400]{1,0:T(8,128)(2,1)S(1)}, bf16[40,6400]{1,0:T(8,128)(2,1)S(1)}, u32[]{:S(2)}, u32[]{:S(2)}) collective-permute-start(bf16[40,6400]{1,0:T(8,128)(2,1)S(1)} %collective-permute-done.13), channel_id=1, source_target_pairs={{1,0},{2,3},{5,4},{6,7},{9,8},{10,11},{13,12},{14,15},{17,16},{18,... | collective-permute-start | bytes 1536008 | tf_op jit(solution)/shard_map/ppermute | solution.py:96
  84.6 58.1 %collective-permute-start.26 = (bf16[40,25600]{1,0:T(8,128)(2,1)}, bf16[40,25600]{1,0:T(8,128)(2,1)}, u32[]{:S(2)}, u32[]{:S(2)}) collective-permute-start(bf16[40,25600]{1,0:T(8,128)(2,1)} %pick.3.refs_0_), channel_id=1, source_target_pairs={{4,2},{5,3},{2,4},{3,5},{12,10},{13,11},{10,12},{11,13},{20,18},{2... | collective-permute-start | bytes 6144008 | tf_op jit(solution)/shard_map/ppermute | solution.py:96
  104.6 17.1 %copy-start = (bf16[2,40,6400]{2,1,0:T(8,128)(2,1)}, bf16[2,40,6400]{2,1,0:T(8,128)(2,1)S(1)}, u32[]{:S(2)}) copy-start(bf16[2,40,6400]{2,1,0:T(8,128)(2,1)S(1)} %pad_maximum_fusion.refs_6_.refs_10_.refs_2_.refs_7_) | copy-start | bytes 3072004
  104.6 20.0 %collective-permute-start.20 = (bf16[2,40,6400]{2,1,0:T(8,128)(2,1)S(1)}, bf16[2,40,6400]{2,1,0:T(8,128)(2,1)S(1)}, u32[]{:S(2)}, u32[]{:S(2)}) collective-permute-start(bf16[2,40,6400]{2,1,0:T(8,128)(2,1)S(1)} %pad_maximum_fusion.refs_6_.refs_10_.refs_2_.refs_7_), channel_id=1, source_target_pairs={{0,16},{1,17},{2,18},{3,19},{4,20},{5,21},{6,22},{7,23},{8,24},{9,... | collective-permute-start | bytes 3072008 | tf_op jit(solution)/shard_map/ppermute | solution.py:96
  104.9 25.7 %collective-permute-start.19 = (bf16[2,40,6400]{2,1,0:T(8,128)(2,1)S(1)}, bf16[2,40,6400]{2,1,0:T(8,128)(2,1)S(1)}, u32[]{:S(2)}, u32[]{:S(2)}) collective-permute-start(bf16[2,40,6400]{2,1,0:T(8,128)(2,1)S(1)} %pad_maximum_fusion.refs_6_.refs_10_.refs_2_.refs_7_), channel_id=1, source_target_pairs={{0,8},{1,9},{2,10},{3,11},{4,12},{5,13},{6,14},{7,15},{8,0},{9,1},... | collective-permute-start | bytes 3072008 | tf_op jit(solution)/shard_map/ppermute | solution.py:96
  106.5 25.0 %collective-permute-start.22 = (bf16[40,16000]{1,0:T(8,128)(2,1)}, bf16[40,16000]{1,0:T(8,128)(2,1)}, u32[]{:S(2)}, u32[]{:S(2)}) collective-permute-start(bf16[40,16000]{1,0:T(8,128)(2,1)} %collective-permute-done.5.refs_1_.refs_4_), channel_id=1, source_target_pairs={{0,4},{1,5},{2,6},{3,7},{4,0},{5,1},{6,2},{7,3},{8,12},{9,13},{10,... | collective-permute-start | bytes 3840008 | tf_op jit(solution)/shard_map/ppermute | solution.py:96
  121.7 9.8 %collective-permute-start.23 = (bf16[40,6400]{1,0:T(8,128)(2,1)S(1)}, bf16[40,6400]{1,0:T(8,128)(2,1)S(1)}, u32[]{:S(2)}, u32[]{:S(2)}) collective-permute-start(bf16[40,6400]{1,0:T(8,128)(2,1)S(1)} %collective-permute-done.18.refs_2_.refs_5_), channel_id=1, source_target_pairs={{0,4},{1,5},{2,6},{3,7},{4,0},{5,1},{6,2},{7,3},{8,12},{9,13},{10,... | collective-permute-start | bytes 1536008 | tf_op jit(solution)/shard_map/ppermute | solution.py:96
  124.6 18.0 %copy-start.1 = (bf16[2,40,6400]{2,1,0:T(8,128)(2,1)}, bf16[2,40,6400]{2,1,0:T(8,128)(2,1)S(1)}, u32[]{:S(2)}) copy-start(bf16[2,40,6400]{2,1,0:T(8,128)(2,1)S(1)} %collective-permute-done.20.refs_8_.refs_12_.refs_4_.refs_9_) | copy-start | bytes 3072004
  124.6 6.8 %collective-permute-start.21 = (bf16[40,3200]{1,0:T(8,128)(2,1)}, bf16[40,3200]{1,0:T(8,128)(2,1)S(1)}, u32[]{:S(2)}, u32[]{:S(2)}) collective-permute-start(bf16[40,3200]{1,0:T(8,128)(2,1)} %collective-permute-done.1.refs_0_.refs_3_), channel_id=1, source_target_pairs={{0,4},{1,5},{2,6},{3,7},{4,0},{5,1},{6,2},{7,3},{8,12},{9,13},{10,... | collective-permute-start | bytes 768008 | tf_op jit(solution)/shard_map/ppermute | solution.py:96
  132.2 13.5 %collective-permute-start.24 = (bf16[2,40,3200]{2,1,0:T(8,128)(2,1)}, bf16[2,40,3200]{2,1,0:T(8,128)(2,1)S(1)}, u32[]{:S(2)}, u32[]{:S(2)}) collective-permute-start(bf16[2,40,3200]{2,1,0:T(8,128)(2,1)} %slice.42), channel_id=1, source_target_pairs={{0,16},{1,17},{2,18},{3,19},{4,20},{5,21},{6,22},{7,23},{8,24},{9,... | collective-permute-start | bytes 1536008 | tf_op jit(solution)/shard_map/ppermute | solution.py:96
  132.4 13.2 %collective-permute-start.25 = (bf16[2,40,3200]{2,1,0:T(8,128)(2,1)}, bf16[2,40,3200]{2,1,0:T(8,128)(2,1)S(1)}, u32[]{:S(2)}, u32[]{:S(2)}) collective-permute-start(bf16[2,40,3200]{2,1,0:T(8,128)(2,1)} %slice.43), channel_id=1, source_target_pairs={{0,8},{1,9},{2,10},{3,11},{4,12},{5,13},{6,14},{7,15},{8,0},{9,1},... | collective-permute-start | bytes 1536008 | tf_op jit(solution)/shard_map/ppermute | solution.py:96
  145.7 10.4 %collective-permute-start.27 = (bf16[40,25600]{1,0:T(8,128)(2,1)}, bf16[40,25600]{1,0:T(8,128)(2,1)}, u32[]{:S(2)}, u32[]{:S(2)}) collective-permute-start(bf16[40,25600]{1,0:T(8,128)(2,1)} %collective-permute-done.26.refs_4_), channel_id=1, source_target_pairs={{0,4},{1,5},{2,6},{3,7},{4,0},{5,1},{6,2},{7,3},{8,12},{9,13},{10,... | collective-permute-start | bytes 6144008 | tf_op jit(solution)/shard_map/ppermute | solution.py:96
  191.0 2.9 collective-permute-start.28
  191.8 18.8 %collective-permute-start.30 = (bf16[40,15360]{1,0:T(8,128)(2,1)}, bf16[40,15360]{1,0:T(8,128)(2,1)S(1)}, u32[]{:S(2)}, u32[]{:S(2)}) collective-permute-start(bf16[40,15360]{1,0:T(8,128)(2,1)} %get-tuple-element.137), channel_id=1, source_target_pairs={{0,4},{1,5},{2,6},{3,7},{4,0},{5,1},{6,2},{7,3},{8,12},{9,13},{10,... | collective-permute-start | bytes 3686408 | tf_op jit(solution)/shard_map/ppermute | solution.py:96
  196.2 21.7 %collective-permute-start.29 = (bf16[40,10240]{1,0:T(8,128)(2,1)}, bf16[40,10240]{1,0:T(8,128)(2,1)}, u32[]{:S(2)}, u32[]{:S(2)}) collective-permute-start(bf16[40,10240]{1,0:T(8,128)(2,1)} %add_convert_fusion.1), channel_id=1, source_target_pairs={{0,3},{1,0},{2,5},{3,6},{4,1},{5,2},{6,7},{7,4},{8,11},{9,8},{10,1... | collective-permute-start | bytes 2457608 | tf_op jit(solution)/shard_map/ppermute | solution.py:96
  205.9 21.6 %collective-permute-start.34 = (bf16[40,6400]{1,0:T(8,128)(2,1)}, bf16[40,6400]{1,0:T(8,128)(2,1)}, u32[]{:S(2)}, u32[]{:S(2)}) collective-permute-start(bf16[40,6400]{1,0:T(8,128)(2,1)} %get-tuple-element.147), channel_id=1, source_target_pairs={{0,4},{1,5},{2,6},{3,7},{4,0},{5,1},{6,2},{7,3},{8,12},{9,13},{10,... | collective-permute-start | bytes 1536008 | tf_op jit(solution)/shard_map/ppermute | solution.py:96
  210.0 22.0 %collective-permute-start.36 = (bf16[40,6400]{1,0:T(8,128)(2,1)}, bf16[40,6400]{1,0:T(8,128)(2,1)}, u32[]{:S(2)}, u32[]{:S(2)}) collective-permute-start(bf16[40,6400]{1,0:T(8,128)(2,1)} %get-tuple-element.149), channel_id=1, source_target_pairs={{0,4},{1,5},{2,6},{3,7},{4,0},{5,1},{6,2},{7,3},{8,12},{9,13},{10,... | collective-permute-start | bytes 1536008 | tf_op jit(solution)/shard_map/ppermute | solution.py:96
  210.1 28.2 %collective-permute-start.38 = (bf16[40,6400]{1,0:T(8,128)(2,1)}, bf16[40,6400]{1,0:T(8,128)(2,1)}, u32[]{:S(2)}, u32[]{:S(2)}) collective-permute-start(bf16[40,6400]{1,0:T(8,128)(2,1)} %get-tuple-element.151), channel_id=1, source_target_pairs={{0,4},{1,5},{2,6},{3,7},{4,0},{5,1},{6,2},{7,3},{8,12},{9,13},{10,... | collective-permute-start | bytes 1536008 | tf_op jit(solution)/shard_map/ppermute | solution.py:96
  210.6 32.0 %collective-permute-start.32 = (bf16[40,6400]{1,0:T(8,128)(2,1)}, bf16[40,6400]{1,0:T(8,128)(2,1)}, u32[]{:S(2)}, u32[]{:S(2)}) collective-permute-start(bf16[40,6400]{1,0:T(8,128)(2,1)} %get-tuple-element.142), channel_id=1, source_target_pairs={{0,4},{1,5},{2,6},{3,7},{4,0},{5,1},{6,2},{7,3},{8,12},{9,13},{10,... | collective-permute-start | bytes 1536008 | tf_op jit(solution)/shard_map/ppermute | solution.py:96
  217.9 32.0 %collective-permute-start.31 = (bf16[40,15360]{1,0:T(8,128)(2,1)S(1)}, bf16[40,15360]{1,0:T(8,128)(2,1)}, u32[]{:S(2)}, u32[]{:S(2)}) collective-permute-start(bf16[40,15360]{1,0:T(8,128)(2,1)S(1)} %add_convert_fusion), channel_id=1, source_target_pairs={{0,3},{1,0},{2,5},{3,6},{4,1},{5,2},{6,7},{7,4},{8,11},{9,8},{10,1... | collective-permute-start | bytes 3686408 | tf_op jit(solution)/shard_map/ppermute | solution.py:96
  229.7 43.6 %collective-permute-start.35 = (bf16[40,6400]{1,0:T(8,128)(2,1)}, bf16[40,6400]{1,0:T(8,128)(2,1)}, u32[]{:S(2)}, u32[]{:S(2)}) collective-permute-start(bf16[40,6400]{1,0:T(8,128)(2,1)} %add_convert_fusion.4.refs_2_), channel_id=1, source_target_pairs={{2,4},{3,5},{4,2},{5,3},{10,12},{11,13},{12,10},{13,11},{18,20},{1... | collective-permute-start | bytes 1536008 | tf_op jit(solution)/shard_map/ppermute | solution.py:96
  234.1 44.7 %collective-permute-start.37 = (bf16[40,6400]{1,0:T(8,128)(2,1)}, bf16[40,6400]{1,0:T(8,128)(2,1)}, u32[]{:S(2)}, u32[]{:S(2)}) collective-permute-start(bf16[40,6400]{1,0:T(8,128)(2,1)} %add_convert_fusion.3.refs_3_), channel_id=1, source_target_pairs={{2,4},{3,5},{4,2},{5,3},{10,12},{11,13},{12,10},{13,11},{18,20},{1... | collective-permute-start | bytes 1536008 | tf_op jit(solution)/shard_map/ppermute | solution.py:96
  240.3 44.1 %collective-permute-start.39 = (bf16[40,6400]{1,0:T(8,128)(2,1)}, bf16[40,6400]{1,0:T(8,128)(2,1)}, u32[]{:S(2)}, u32[]{:S(2)}) collective-permute-start(bf16[40,6400]{1,0:T(8,128)(2,1)} %add_convert_fusion.2.refs_4_), channel_id=1, source_target_pairs={{2,4},{3,5},{4,2},{5,3},{10,12},{11,13},{12,10},{13,11},{18,20},{1... | collective-permute-start | bytes 1536008 | tf_op jit(solution)/shard_map/ppermute | solution.py:96
  244.6 45.3 %collective-permute-start.33 = (bf16[40,6400]{1,0:T(8,128)(2,1)}, bf16[40,6400]{1,0:T(8,128)(2,1)}, u32[]{:S(2)}, u32[]{:S(2)}) collective-permute-start(bf16[40,6400]{1,0:T(8,128)(2,1)} %add_convert_fusion.5.refs_1_), channel_id=1, source_target_pairs={{2,4},{3,5},{4,2},{5,3},{10,12},{11,13},{12,10},{13,11},{18,20},{1... | collective-permute-start | bytes 1536008 | tf_op jit(solution)/shard_map/ppermute | solution.py:96
  (11 other events, 95.7 us)
where the time goes:
time: 294 us; the launch traced here: 293 us
  Pallas kernels  101 us (34%)
  waiting for transfers between devices  97 us (33%)
  starting transfers between devices  66.1 us (22%)
  other arithmetic  15.7 us (5%)
  local copies, waits for them, and re-layouts  10.3 us (4%)
  between operations  3.34 us (1%)
    ppermute x40, waiting for transfers between devices, move(): lax.ppermute(x, ('band', 'grid'), [(place(*a), place(*b)) for a, b in rou...  97 us
    ppermute x40, starting transfers between devices, move(): lax.ppermute(x, ('band', 'grid'), [(place(*a), place(*b)) for a, b in rou...  66.1 us
    pallas_call x1, Pallas kernels, central(): pl.pallas_call(functools.partial(central_kernel, home, direct), out_shape...  34.9 us
    pallas_call x3, Pallas kernels, forward(): pl.pallas_call(functools.partial(forward_kernel, place, first, len(target...  27.9 us
    pallas_call x2, Pallas kernels, backward(): pl.pallas_call(functools.partial(backward_kernel, places, first, parts),...  19.3 us
    convert_element_type x6, other arithmetic, add(): return (a.astype(jnp.float32) + b.astype(jnp.float32)).astype(jnp.bfloat16)  10.7 us
    pallas_call x2, Pallas kernels, pick(): pl.pallas_call(functools.partial(pick_kernel, which), out_shape=[jax.Shap...  8.57 us
    pallas_call x2, Pallas kernels, put(): pl.pallas_call(functools.partial(put_kernel, len(choices), len(before)),...  6.33 us
  transfers between devices with their start and end apart: 40, of which 17 were waited for; matrix products, arithmetic and copies ran while one was open for 9% of the time, Pallas kernels for 20%

commit v1 on v0

--- a/solution.py
+++ b/solution.py
@@ -255,7 +255,7 @@
 def transform_in(source, target, windows, cas, turned, out):
     planes, points = target.shape
     extent = cas.shape[0]
-    step = 10
+    step = 20
     block = quad * extent
 
     @pl.loop(0, points // block // step)
@@ -271,10 +271,10 @@
                 y = (i * step + j) * quad + r
                 put_both(turned, pl.ds(y, planes, stride=turned_pitch), along_z[j * planes : (j + 1) * planes])
 
-    @pl.loop(0, planes // 8)
+    @pl.loop(0, planes // 20)
     def _(i):
-        for j in range(8):
-            x = i * 8 + j
+        for j in range(20):
+            x = i * 20 + j
             along_z = both(turned, pl.ds(x * turned_pitch, extent)).astype(jnp.bfloat16)
             put_both(out, pl.ds(x, extent, stride=plane_pitch), dot(cas[...], along_z))
 
@@ -283,7 +283,7 @@
     extent = square.shape[0]
     planes = extent // ring
     strength = (extent * spacing) ** 2 / math.pi
-    rows = 16
+    rows = 32
 
     @pl.loop(0, extent // rows)
     def _(step):
@@ -307,10 +307,10 @@
     planes, points = source.shape
     extent = cas.shape[0]
 
-    @pl.loop(0, planes // 8)
+    @pl.loop(0, planes // 20)
     def _(i):
-        for j in range(8):
-            x = i * 8 + j
+        for j in range(20):
+            x = i * 20 + j
             column_x = both(back_x, pl.ds(x, extent, stride=plane_pitch)).astype(jnp.bfloat16)
             put_both(turned, pl.ds(x * turned_pitch, extent), dot(cas[...], column_x))
 
@@ -318,7 +318,7 @@
     begin = 0
     for out in outs:
         blocks = out.shape[1] // block
-        step = 5 if blocks % 5 == 0 else 4
+        step = 10 if blocks % 10 == 0 else 8
 
         @pl.loop(0, blocks // step)
         def _(i, begin=begin, step=step, out=out):

time: 294 us -> 288 us (0.980)
  Pallas kernels: 101 us -> 88.7 us
  waiting for transfers between devices: 97 us -> 103 us
    ppermute x40, waiting for transfers between devices: 97 us -> 103 us  [move(): lax.ppermute(x, ('band', 'grid'), [(place(*a), place(*b)) for a, b in rou...]
    pallas_call x1, Pallas kernels: 34.9 us -> 29.7 us  [central(): pl.pallas_call(functools.partial(central_kernel, home, direct), out_shape...]
    pallas_call x2, Pallas kernels: 19.3 us -> 15.1 us  [backward(): pl.pallas_call(functools.partial(backward_kernel, places, first, parts),...]
  transfers between devices with their start and end apart: 40 -> 40, of which waited for: 17 -> 18; matrix products, arithmetic and copies ran while one was open for 9% -> 9% of each run, Pallas kernels for 20% -> 18%
where the time goes in v1:
time: 288 us; the launch traced here: 287 us
  waiting for transfers between devices  103 us (36%)
  Pallas kernels  88.7 us (31%)
  starting transfers between devices  66.3 us (23%)
  other arithmetic  15.7 us (5%)
  local copies, waits for them, and re-layouts  10.3 us (4%)
  between operations  3.36 us (1%)
    ppermute x40, waiting for transfers between devices, move(): lax.ppermute(x, ('band', 'grid'), [(place(*a), place(*b)) for a, b in rou...  103 us
    ppermute x40, starting transfers between devices, move(): lax.ppermute(x, ('band', 'grid'), [(place(*a), place(*b)) for a, b in rou...  66.3 us
    pallas_call x1, Pallas kernels, central(): pl.pallas_call(functools.partial(central_kernel, home, direct), out_shape...  29.7 us
    pallas_call x3, Pallas kernels, forward(): pl.pallas_call(functools.partial(forward_kernel, place, first, len(target...  25.4 us
    pallas_call x2, Pallas kernels, backward(): pl.pallas_call(functools.partial(backward_kernel, places, first, parts),...  15.1 us
    convert_element_type x6, other arithmetic, add(): return (a.astype(jnp.float32) + b.astype(jnp.float32)).astype(jnp.bfloat16)  10.7 us
    pallas_call x2, Pallas kernels, pick(): pl.pallas_call(functools.partial(pick_kernel, which), out_shape=[jax.Shap...  8.57 us
    pallas_call x2, Pallas kernels, put(): pl.pallas_call(functools.partial(put_kernel, len(choices), len(before)),...  6.33 us
  transfers between devices with their start and end apart: 40, of which 18 were waited for; matrix products, arithmetic and copies ran while one was open for 9% of the time, Pallas kernels for 18%

profile of v1, /device:TPU:1, one launch (start us, length us, event | category | flops | bytes accessed | tf_op | source)
XLA Modules:
  0.0 287.1 jit_solution(8708125651199595111)
XLA Ops:
  0.0 4.9 %pick.2 = (bf16[40,25600]{1,0:T(8,128)(2,1)}, bf16[40,3200]{1,0:T(8,128)(2,1)}, bf16[40,16000]{1,0:T(8,128)(2,1)}, bf16[40,6400]{1,0:T(8,128)(2,1)}) custom-call(s32[2]{0:T(128)} %source_index.5, bf16[2,40,25600]{2,1,0:T(8,128)(2,1)} %orbitals.4), custom_call_target="tpu_custom_call" | custom-call | flops 1000000 | bytes 10000 | tf_op jit(solution)/shard_map/pick/pallas_call | solution.py:419
  5.0 4.7 %collective-permute-start.1 = (bf16[40,3200]{1,0:T(8,128)(2,1)}, bf16[40,3200]{1,0:T(8,128)(2,1)}, u32[]{:S(2)}, u32[]{:S(2)}) collective-permute-start(bf16[40,3200]{1,0:T(8,128)(2,1)} %get-tuple-element.86), channel_id=1, source_target_pairs={{3,0},{0,1},{5,2},{6,3},{1,4},{2,5},{7,6},{4,7},{11,8},{8,9},{13,1... | collective-permute-start | bytes 768008 | tf_op jit(solution)/shard_map/ppermute | solution.py:96
  9.7 3.5 %cut.1 = (bf16[40,6400]{1,0:T(8,128)(2,1)}, bf16[40,6400]{1,0:T(8,128)(2,1)}, bf16[40,6400]{1,0:T(8,128)(2,1)}, bf16[40,6400]{1,0:T(8,128)(2,1)}) custom-call(s32[2]{0:T(128)} %source_index.5, bf16[2,40,25600]{2,1,0:T(8,128)(2,1)} %orbitals.4, bf16[40,25600]{1,0:T(8,128)(2,1)} %collective-permute-done.crossed), custom_call_target="tpu_custom_call" | custom-call | flops 1000000 | bytes 10000 | tf_op jit(solution)/shard_map/cut/pallas_call | solution.py:433
  14.5 3.7 %collective-permute-start.5 = (bf16[40,16000]{1,0:T(8,128)(2,1)}, bf16[40,16000]{1,0:T(8,128)(2,1)}, u32[]{:S(2)}, u32[]{:S(2)}) collective-permute-start(bf16[40,16000]{1,0:T(8,128)(2,1)} %get-tuple-element.94), channel_id=1, source_target_pairs={{3,0},{0,1},{5,2},{6,3},{1,4},{2,5},{7,6},{4,7},{11,8},{8,9},{13,1... | collective-permute-start | bytes 3840008 | tf_op jit(solution)/shard_map/ppermute | solution.py:96
  21.9 1.3 dynamic_slice.3
  28.2 1.5 multiply_convert_fusion
  29.8 3.7 %pick.3.refs_0_ = bf16[40,25600]{1,0:T(8,128)(2,1)} custom-call(s32[2]{0:T(128)} %source_index.5, bf16[2,40,25600]{2,1,0:T(8,128)(2,1)} %orbitals.4), custom_call_target="tpu_custom_call" | custom-call | flops 1000000 | bytes 10000 | tf_op jit(solution)/shard_map/pick/pallas_call | solution.py:419
  33.5 11.0 %collective-permute-done.3 = bf16[40,6400]{1,0:T(8,128)(2,1)S(1)} collective-permute-done((bf16[40,6400]{1,0:T(8,128)(2,1)}, bf16[40,6400]{1,0:T(8,128)(2,1)S(1)}, u32[]{:S(2)}, u32[]{:S(2)}) %collective-permute-start.3) | collective-permute-done | bytes 512032 | tf_op jit(solution)/shard_map/ppermute | solution.py:96
  45.8 1.9 collective-permute-start.10
  47.8 1.3 collective-permute-start.9
  51.1 1.3 collective-permute-start.6
  55.6 5.6 %collective-permute-done.9 = bf16[40,6400]{1,0:T(8,128)(2,1)S(1)} collective-permute-done((bf16[40,6400]{1,0:T(8,128)(2,1)S(1)}, bf16[40,6400]{1,0:T(8,128)(2,1)S(1)}, u32[]{:S(2)}, u32[]{:S(2)}) %collective-permute-start.9) | collective-permute-done | bytes 512032 | tf_op jit(solution)/shard_map/ppermute | solution.py:96
  62.1 1.6 collective-permute-done.6
  65.0 1.3 collective-permute-start.14
  66.4 9.9 %collective-permute-done.12 = bf16[40,6400]{1,0:T(8,128)(2,1)S(1)} collective-permute-done((bf16[40,6400]{1,0:T(8,128)(2,1)S(1)}, bf16[40,6400]{1,0:T(8,128)(2,1)S(1)}, u32[]{:S(2)}, u32[]{:S(2)}) %collective-permute-start.12) | collective-permute-done | bytes 512032 | tf_op jit(solution)/shard_map/ppermute | solution.py:96
  76.5 2.8 collective-permute-done.14
  81.8 1.5 collective-permute-start.18
  83.3 1.3 collective-permute-start.15
  84.6 9.0 %collective-permute-start.26 = (bf16[40,25600]{1,0:T(8,128)(2,1)}, bf16[40,25600]{1,0:T(8,128)(2,1)}, u32[]{:S(2)}, u32[]{:S(2)}) collective-permute-start(bf16[40,25600]{1,0:T(8,128)(2,1)} %pick.3.refs_0_), channel_id=1, source_target_pairs={{4,2},{5,3},{2,4},{3,5},{12,10},{13,11},{10,12},{11,13},{20,18},{2... | collective-permute-start | bytes 6144008 | tf_op jit(solution)/shard_map/ppermute | solution.py:96
  93.6 10.8 %collective-permute-done.15 = bf16[40,6400]{1,0:T(8,128)(2,1)S(1)} collective-permute-done((bf16[40,6400]{1,0:T(8,128)(2,1)S(1)}, bf16[40,6400]{1,0:T(8,128)(2,1)S(1)}, u32[]{:S(2)}, u32[]{:S(2)}) %collective-permute-start.15) | collective-permute-done | bytes 512032 | tf_op jit(solution)/shard_map/ppermute | solution.py:96
  106.5 5.1 %collective-permute-start.22 = (bf16[40,16000]{1,0:T(8,128)(2,1)}, bf16[40,16000]{1,0:T(8,128)(2,1)}, u32[]{:S(2)}, u32[]{:S(2)}) collective-permute-start(bf16[40,16000]{1,0:T(8,128)(2,1)} %collective-permute-done.5.refs_1_.refs_4_), channel_id=1, source_target_pairs={{0,4},{1,5},{2,6},{3,7},{4,0},{5,1},{6,2},{7,3},{8,12},{9,13},{10,... | collective-permute-start | bytes 3840008 | tf_op jit(solution)/shard_map/ppermute | solution.py:96
  112.4 8.4 %forward.3.refs_0_ = f32[2,6560,128]{2,1,0:T(8,128)} custom-call(s32[6]{0:T(128)} %stack.100.flags, bf16[40,25600]{1,0:T(8,128)(2,1)} %pick.3.refs_0_, bf16[40,25600]{1,0:T(8,128)(2,1)} %collective-permute-done.10.refs_1_, bf16[1,40,6400]{2,1,0:T(8,128)(2,1)} %bitcast.37, bf16[1,40,6400]{2,1,0:T(8,128)(2,1)} %bitcast.43, bf16[1,40,6400]{2,1,0:T(8,128)(2,1)} %bitcast.40, ...), custom_call_target="tpu_custom_call" | custom-call | flops 1000000 | bytes 10000 | tf_op jit(solution)/shard_map/forward/pallas_call | solution.py:471
  120.9 3.7 %collective-permute-done.20.refs_8_.refs_12_.refs_4_.refs_9_ = bf16[2,40,6400]{2,1,0:T(8,128)(2,1)S(1)} collective-permute-done((bf16[2,40,6400]{2,1,0:T(8,128)(2,1)S(1)}, bf16[2,40,6400]{2,1,0:T(8,128)(2,1)S(1)}, u32[]{:S(2)}, u32[]{:S(2)}) %collective-permute-start.20) | collective-permute-done | bytes 1024032 | tf_op jit(solution)/shard_map/ppermute | solution.py:96
  124.6 5.1 %collective-permute-start.21 = (bf16[40,3200]{1,0:T(8,128)(2,1)}, bf16[40,3200]{1,0:T(8,128)(2,1)S(1)}, u32[]{:S(2)}, u32[]{:S(2)}) collective-permute-start(bf16[40,3200]{1,0:T(8,128)(2,1)} %collective-permute-done.1.refs_0_.refs_3_), channel_id=1, source_target_pairs={{0,4},{1,5},{2,6},{3,7},{4,0},{5,1},{6,2},{7,3},{8,12},{9,13},{10,... | collective-permute-start | bytes 768008 | tf_op jit(solution)/shard_map/ppermute | solution.py:96
  133.3 8.6 %forward.4.refs_1_ = f32[2,6560,128]{2,1,0:T(8,128)} custom-call(s32[6]{0:T(128)} %stack.100.flags, bf16[40,3200]{1,0:T(8,128)(2,1)} %collective-permute-done.1.refs_0_.refs_3_, bf16[40,16000]{1,0:T(8,128)(2,1)} %collective-permute-done.5.refs_1_.refs_4_, bf16[40,6400]{1,0:T(8,128)(2,1)} %copy-done.10, bf16[40,3200]{1,0:T(8,128)(2,1)} %copy-done.14, ...), custom_call_target="tpu_custom_call" | custom-call | flops 1000000 | bytes 10000 | tf_op jit(solution)/shard_map/forward/pallas_call | solution.py:471
  141.9 3.8 %collective-permute-done.24.refs_9_.refs_13_.refs_5_.refs_10_ = bf16[2,40,3200]{2,1,0:T(8,128)(2,1)S(1)} collective-permute-done((bf16[2,40,3200]{2,1,0:T(8,128)(2,1)}, bf16[2,40,3200]{2,1,0:T(8,128)(2,1)S(1)}, u32[]{:S(2)}, u32[]{:S(2)}) %collective-permute-start.24) | collective-permute-done | bytes 512032 | tf_op jit(solution)/shard_map/ppermute | solution.py:96
  146.7 8.5 %forward.5.refs_2_ = f32[2,6560,128]{2,1,0:T(8,128)} custom-call(s32[6]{0:T(128)} %stack.100.flags, bf16[40,3200]{1,0:T(8,128)(2,1)} %copy-done.14, bf16[40,16000]{1,0:T(8,128)(2,1)} %collective-permute-done.22.refs_4_.refs_1_, bf16[40,6400]{1,0:T(8,128)(2,1)} %copy-done.11, bf16[40,3200]{1,0:T(8,128)(2,1)} %collective-permute-done.1.refs_0_.refs_3_, ...), custom_call_target="tpu_custom_call" | custom-call | flops 1000000 | bytes 10000 | tf_op jit(solution)/shard_map/forward/pallas_call | solution.py:471
  155.2 29.7 %central.1 = (bf16[40,10240]{1,0:T(8,128)(2,1)}, bf16[40,15360]{1,0:T(8,128)(2,1)}, bf16[40,10240]{1,0:T(8,128)(2,1)}, bf16[40,15360]{1,0:T(8,128)(2,1)}, f32[2,...) custom-call(s32[6]{0:T(128)} %stack.100.flags, f32[2,6560,128]{2,1,0:T(8,128)} %forward.3.refs_0_, ...), custom_call_target="tpu_custom_call" | custom-call | flops 1000000 | bytes 10000 | tf_op jit(solution)/shard_map/central/pallas_call | solution.py:495
  185.9 2.1 collective-permute-done.28
  187.9 2.2 add_convert_fusion.1
  190.2 7.6 %backward.2 = (bf16[40,6400]{1,0:T(8,128)(2,1)}, bf16[40,6400]{1,0:T(8,128)(2,1)}, bf16[40,6400]{1,0:T(8,128)(2,1)}, bf16[40,6400]{1,0:T(8,128)(2,1)}) custom-call(s32[6]{0:T(128)} %stack.100.flags, f32[2,6560,128]{2,1,0:T(8,128)} %get-tuple-element.144.refs_0_.refs_1_, f32[2,6560,128]{2,1,0:T(8,128)} %get-tuple-element.143.refs_1_.refs_0_, ...), custom_call_target="tpu_custom_call" | custom-call | flops 1000000 | bytes 10000 | tf_op jit(solution)/shard_map/backward/pallas_call | solution.py:520
  197.8 4.1 %collective-permute-start.34 = (bf16[40,6400]{1,0:T(8,128)(2,1)}, bf16[40,6400]{1,0:T(8,128)(2,1)}, u32[]{:S(2)}, u32[]{:S(2)}) collective-permute-start(bf16[40,6400]{1,0:T(8,128)(2,1)} %get-tuple-element.147), channel_id=1, source_target_pairs={{0,4},{1,5},{2,6},{3,7},{4,0},{5,1},{6,2},{7,3},{8,12},{9,13},{10,... | collective-permute-start | bytes 1536008 | tf_op jit(solution)/shard_map/ppermute | solution.py:96
  202.8 9.1 %collective-permute-done.29.refs_0_ = bf16[40,10240]{1,0:T(8,128)(2,1)} collective-permute-done((bf16[40,10240]{1,0:T(8,128)(2,1)}, bf16[40,10240]{1,0:T(8,128)(2,1)}, u32[]{:S(2)}, u32[]{:S(2)}) %collective-permute-start.29) | collective-permute-done | bytes 819232 | tf_op jit(solution)/shard_map/ppermute | solution.py:96
  211.9 7.5 %backward.3 = (bf16[40,6400]{1,0:T(8,128)(2,1)}, bf16[40,6400]{1,0:T(8,128)(2,1)}, bf16[40,6400]{1,0:T(8,128)(2,1)}, bf16[40,6400]{1,0:T(8,128)(2,1)}) custom-call(s32[6]{0:T(128)} %stack.100.flags, f32[2,6560,128]{2,1,0:T(8,128)} %get-tuple-element.143.refs_1_.refs_0_, f32[2,6560,128]{2,1,0:T(8,128)} %get-tuple-element.144.refs_0_.refs_1_, ...), custom_call_target="tpu_custom_call" | custom-call | flops 1000000 | bytes 10000 | tf_op jit(solution)/shard_map/backward/pallas_call | solution.py:520
  219.4 2.2 add_convert_fusion.4.refs_2_
  221.6 2.3 collective-permute-start.35
  223.9 2.1 add_convert_fusion.3.refs_3_
  226.0 4.2 %collective-permute-start.37 = (bf16[40,6400]{1,0:T(8,128)(2,1)}, bf16[40,6400]{1,0:T(8,128)(2,1)}, u32[]{:S(2)}, u32[]{:S(2)}) collective-permute-start(bf16[40,6400]{1,0:T(8,128)(2,1)} %add_convert_fusion.3.refs_3_), channel_id=1, source_target_pairs={{2,4},{3,5},{4,2},{5,3},{10,12},{11,13},{12,10},{13,11},{18,20},{1... | collective-permute-start | bytes 1536008 | tf_op jit(solution)/shard_map/ppermute | solution.py:96
  230.2 2.0 add_convert_fusion.2.refs_4_
  232.2 2.3 collective-permute-start.39
  234.5 2.0 add_convert_fusion.5.refs_1_
  236.4 4.2 %collective-permute-start.33 = (bf16[40,6400]{1,0:T(8,128)(2,1)}, bf16[40,6400]{1,0:T(8,128)(2,1)}, u32[]{:S(2)}, u32[]{:S(2)}) collective-permute-start(bf16[40,6400]{1,0:T(8,128)(2,1)} %add_convert_fusion.5.refs_1_), channel_id=1, source_target_pairs={{2,4},{3,5},{4,2},{5,3},{10,12},{11,13},{12,10},{13,11},{18,20},{1... | collective-permute-start | bytes 1536008 | tf_op jit(solution)/shard_map/ppermute | solution.py:96
  242.5 3.3 %put.2.refs_0_ = bf16[2,40,25600]{2,1,0:T(8,128)(2,1)} custom-call(s32[2]{0:T(128)} %pad_add_fusion.1.flags, bf16[40,10240]{1,0:T(8,128)(2,1)} %collective-permute-done.29.refs_0_, bf16[40,15360]{1,0:T(8,128)(2,1)} %collective-permute-done.31.refs_1_), custom_call_target="tpu_custom_call" | custom-call | flops 1000000 | bytes 10000 | tf_op jit(solution)/shard_map/put/pallas_call | solution.py:450
  245.8 21.6 %collective-permute-done.35.refs_6_ = bf16[40,6400]{1,0:T(8,128)(2,1)} collective-permute-done((bf16[40,6400]{1,0:T(8,128)(2,1)}, bf16[40,6400]{1,0:T(8,128)(2,1)}, u32[]{:S(2)}, u32[]{:S(2)}) %collective-permute-start.35) | collective-permute-done | bytes 512032 | tf_op jit(solution)/shard_map/ppermute | solution.py:96
  267.4 5.5 %collective-permute-done.37.refs_7_ = bf16[40,6400]{1,0:T(8,128)(2,1)} collective-permute-done((bf16[40,6400]{1,0:T(8,128)(2,1)}, bf16[40,6400]{1,0:T(8,128)(2,1)}, u32[]{:S(2)}, u32[]{:S(2)}) %collective-permute-start.37) | collective-permute-done | bytes 512032 | tf_op jit(solution)/shard_map/ppermute | solution.py:96
  272.9 5.5 %collective-permute-done.39.refs_8_ = bf16[40,6400]{1,0:T(8,128)(2,1)} collective-permute-done((bf16[40,6400]{1,0:T(8,128)(2,1)}, bf16[40,6400]{1,0:T(8,128)(2,1)}, u32[]{:S(2)}, u32[]{:S(2)}) %collective-permute-start.39) | collective-permute-done | bytes 512032 | tf_op jit(solution)/shard_map/ppermute | solution.py:96
  278.4 5.5 %collective-permute-done.33.refs_5_ = bf16[40,6400]{1,0:T(8,128)(2,1)} collective-permute-done((bf16[40,6400]{1,0:T(8,128)(2,1)}, bf16[40,6400]{1,0:T(8,128)(2,1)}, u32[]{:S(2)}, u32[]{:S(2)}) %collective-permute-start.33) | collective-permute-done | bytes 512032 | tf_op jit(solution)/shard_map/ppermute | solution.py:96
  283.9 3.1 %put.3 = bf16[2,40,25600]{2,1,0:T(8,128)(2,1)} custom-call(s32[2]{0:T(128)} %pad_add_fusion.flags, bf16[2,40,25600]{2,1,0:T(8,128)(2,1)} %put.2.refs_0_, bf16[40,6400]{1,0:T(8,128)(2,1)} %add_convert_fusion.5.refs_1_, bf16[40,6400]{1,0:T(8,128)(2,1)} %add_convert_fusion.4.refs_2_, ...), custom_call_target="tpu_custom_call", output_to_operand_aliasing={{}: (1, {})} | custom-call | flops 1000000 | bytes 10000 | tf_op jit(solution)/shard_map/put/pallas_call | solution.py:450
  (118 shorter events, 30.1 us)
Async XLA Ops:
  4.9 4.8 %collective-permute-start = (bf16[40,25600]{1,0:T(8,128)(2,1)}, bf16[40,25600]{1,0:T(8,128)(2,1)}, u32[]{:S(2)}, u32[]{:S(2)}) collective-permute-start(bf16[40,25600]{1,0:T(8,128)(2,1)} %get-tuple-element.81), channel_id=1, source_target_pairs={{0,4},{1,5},{2,6},{3,7},{4,0},{5,1},{6,2},{7,3},{8,12},{9,13},{10,... | collective-permute-start | bytes 6144008 | tf_op jit(solution)/shard_map/ppermute | solution.py:96
  5.0 9.6 %collective-permute-start.1 = (bf16[40,3200]{1,0:T(8,128)(2,1)}, bf16[40,3200]{1,0:T(8,128)(2,1)}, u32[]{:S(2)}, u32[]{:S(2)}) collective-permute-start(bf16[40,3200]{1,0:T(8,128)(2,1)} %get-tuple-element.86), channel_id=1, source_target_pairs={{3,0},{0,1},{5,2},{6,3},{1,4},{2,5},{7,6},{4,7},{11,8},{8,9},{13,1... | collective-permute-start | bytes 768008 | tf_op jit(solution)/shard_map/ppermute | solution.py:96
  14.5 31.2 %collective-permute-start.5 = (bf16[40,16000]{1,0:T(8,128)(2,1)}, bf16[40,16000]{1,0:T(8,128)(2,1)}, u32[]{:S(2)}, u32[]{:S(2)}) collective-permute-start(bf16[40,16000]{1,0:T(8,128)(2,1)} %get-tuple-element.94), channel_id=1, source_target_pairs={{3,0},{0,1},{5,2},{6,3},{1,4},{2,5},{7,6},{4,7},{11,8},{8,9},{13,1... | collective-permute-start | bytes 3840008 | tf_op jit(solution)/shard_map/ppermute | solution.py:96
  18.4 15.1 %collective-permute-start.2 = (bf16[40,6400]{1,0:T(8,128)(2,1)}, bf16[40,6400]{1,0:T(8,128)(2,1)S(1)}, u32[]{:S(2)}, u32[]{:S(2)}) collective-permute-start(bf16[40,6400]{1,0:T(8,128)(2,1)} %get-tuple-element.90), channel_id=1, source_target_pairs={{0,8},{1,9},{2,10},{3,11},{4,12},{5,13},{6,14},{7,15},{8,0},{9,1},... | collective-permute-start | bytes 1536008 | tf_op jit(solution)/shard_map/ppermute | solution.py:96
  19.7 24.8 %collective-permute-start.3 = (bf16[40,6400]{1,0:T(8,128)(2,1)}, bf16[40,6400]{1,0:T(8,128)(2,1)S(1)}, u32[]{:S(2)}, u32[]{:S(2)}) collective-permute-start(bf16[40,6400]{1,0:T(8,128)(2,1)} %get-tuple-element.91), channel_id=1, source_target_pairs={{0,16},{1,17},{2,18},{3,19},{4,20},{5,21},{6,22},{7,23},{8,24},{9,... | collective-permute-start | bytes 1536008 | tf_op jit(solution)/shard_map/ppermute | solution.py:96
  20.9 23.6 %collective-permute-start.4 = (bf16[40,6400]{1,0:T(8,128)(2,1)}, bf16[40,6400]{1,0:T(8,128)(2,1)S(1)}, u32[]{:S(2)}, u32[]{:S(2)}) collective-permute-start(bf16[40,6400]{1,0:T(8,128)(2,1)} %get-tuple-element.92), channel_id=1, source_target_pairs={{0,24},{1,25},{2,26},{3,27},{4,28},{5,29},{6,30},{7,31},{8,16},{9,... | collective-permute-start | bytes 1536008 | tf_op jit(solution)/shard_map/ppermute | solution.py:96
  29.8 17.9 %copy-start.17 = (bf16[40,6400]{1,0:T(8,128)(2,1)S(1)}, bf16[40,6400]{1,0:T(8,128)(2,1)}, u32[]{:S(2)}) copy-start(bf16[40,6400]{1,0:T(8,128)(2,1)} %get-tuple-element.96) | copy-start | bytes 1536004
  45.8 18.0 %collective-permute-start.10 = (bf16[40,25600]{1,0:T(8,128)(2,1)}, bf16[40,25600]{1,0:T(8,128)(2,1)}, u32[]{:S(2)}, u32[]{:S(2)}) collective-permute-start(bf16[40,25600]{1,0:T(8,128)(2,1)} %pick.3.refs_0_), channel_id=1, source_target_pairs={{0,4},{1,5},{2,6},{3,7},{4,0},{5,1},{6,2},{7,3},{8,12},{9,13},{10,... | collective-permute-start | bytes 6144008 | tf_op jit(solution)/shard_map/ppermute | solution.py:96
  47.8 28.6 %copy-start.3 = (bf16[40,6400]{1,0:T(8,128)(2,1)}, bf16[40,6400]{1,0:T(8,128)(2,1)S(1)}, u32[]{:S(2)}) copy-start(bf16[40,6400]{1,0:T(8,128)(2,1)S(1)} %select_select_fusion) | copy-start | bytes 1536004
  47.8 13.4 %collective-permute-start.9 = (bf16[40,6400]{1,0:T(8,128)(2,1)S(1)}, bf16[40,6400]{1,0:T(8,128)(2,1)S(1)}, u32[]{:S(2)}, u32[]{:S(2)}) collective-permute-start(bf16[40,6400]{1,0:T(8,128)(2,1)S(1)} %select_select_fusion), channel_id=1, source_target_pairs={{0,16},{1,17},{2,18},{3,19},{4,20},{5,21},{6,22},{7,23},{8,24},{9,... | collective-permute-start | bytes 1536008 | tf_op jit(solution)/shard_map/ppermute | solution.py:96
  49.2 13.0 %collective-permute-start.8 = (bf16[40,6400]{1,0:T(8,128)(2,1)S(1)}, bf16[40,6400]{1,0:T(8,128)(2,1)S(1)}, u32[]{:S(2)}, u32[]{:S(2)}) collective-permute-start(bf16[40,6400]{1,0:T(8,128)(2,1)S(1)} %select_select_fusion), channel_id=1, source_target_pairs={{0,8},{1,9},{2,10},{3,11},{4,12},{5,13},{6,14},{7,15},{8,0},{9,1},... | collective-permute-start | bytes 1536008 | tf_op jit(solution)/shard_map/ppermute | solution.py:96
  50.4 11.8 %collective-permute-start.7 = (bf16[40,6400]{1,0:T(8,128)(2,1)S(1)}, bf16[40,6400]{1,0:T(8,128)(2,1)S(1)}, u32[]{:S(2)}, u32[]{:S(2)}) collective-permute-start(bf16[40,6400]{1,0:T(8,128)(2,1)S(1)} %select_select_fusion), channel_id=1, source_target_pairs={{1,2},{2,1},{5,6},{6,5},{9,10},{10,9},{13,14},{14,13},{17,18},{18,... | collective-permute-start | bytes 1536008 | tf_op jit(solution)/shard_map/ppermute | solution.py:96
  51.1 12.7 %collective-permute-start.6 = (bf16[40,6400]{1,0:T(8,128)(2,1)S(1)}, bf16[40,6400]{1,0:T(8,128)(2,1)S(1)}, u32[]{:S(2)}, u32[]{:S(2)}) collective-permute-start(bf16[40,6400]{1,0:T(8,128)(2,1)S(1)} %select_select_fusion), channel_id=1, source_target_pairs={{0,1},{1,0},{2,3},{3,2},{4,5},{5,4},{6,7},{7,6},{8,9},{9,8},{10,11... | collective-permute-start | bytes 1536008 | tf_op jit(solution)/shard_map/ppermute | solution.py:96
  55.6 26.2 %copy-start.18 = (bf16[40,6400]{1,0:T(8,128)(2,1)S(1)}, bf16[40,6400]{1,0:T(8,128)(2,1)}, u32[]{:S(2)}) copy-start(bf16[40,6400]{1,0:T(8,128)(2,1)} %get-tuple-element.120) | copy-start | bytes 1536004
  61.2 15.3 %copy-start.6 = (bf16[40,6400]{1,0:T(8,128)(2,1)}, bf16[40,6400]{1,0:T(8,128)(2,1)S(1)}, u32[]{:S(2)}) copy-start(bf16[40,6400]{1,0:T(8,128)(2,1)S(1)} %collective-permute-done.9) | copy-start | bytes 1536004
  63.8 15.5 %collective-permute-start.13 = (bf16[40,6400]{1,0:T(8,128)(2,1)S(1)}, bf16[40,6400]{1,0:T(8,128)(2,1)S(1)}, u32[]{:S(2)}, u32[]{:S(2)}) collective-permute-start(bf16[40,6400]{1,0:T(8,128)(2,1)S(1)} %collective-permute-done.6), channel_id=1, source_target_pairs={{1,2},{2,1},{5,6},{6,5},{9,10},{10,9},{13,14},{14,13},{17,18},{18,... | collective-permute-start | bytes 1536008 | tf_op jit(solution)/shard_map/ppermute | solution.py:96
  64.5 11.8 %collective-permute-start.12 = (bf16[40,6400]{1,0:T(8,128)(2,1)S(1)}, bf16[40,6400]{1,0:T(8,128)(2,1)S(1)}, u32[]{:S(2)}, u32[]{:S(2)}) collective-permute-start(bf16[40,6400]{1,0:T(8,128)(2,1)S(1)} %collective-permute-done.6), channel_id=1, source_target_pairs={{0,16},{1,17},{2,18},{3,19},{4,20},{5,21},{6,22},{7,23},{8,24},{9,... | collective-permute-start | bytes 1536008 | tf_op jit(solution)/shard_map/ppermute | solution.py:96
  64.8 11.5 %collective-permute-start.11 = (bf16[40,6400]{1,0:T(8,128)(2,1)S(1)}, bf16[40,6400]{1,0:T(8,128)(2,1)S(1)}, u32[]{:S(2)}, u32[]{:S(2)}) collective-permute-start(bf16[40,6400]{1,0:T(8,128)(2,1)S(1)} %collective-permute-done.6), channel_id=1, source_target_pairs={{0,8},{1,9},{2,10},{3,11},{4,12},{5,13},{6,14},{7,15},{8,0},{9,1},... | collective-permute-start | bytes 1536008 | tf_op jit(solution)/shard_map/ppermute | solution.py:96
  65.0 14.3 %collective-permute-start.14 = (bf16[40,6400]{1,0:T(8,128)(2,1)S(1)}, bf16[40,6400]{1,0:T(8,128)(2,1)S(1)}, u32[]{:S(2)}, u32[]{:S(2)}) collective-permute-start(bf16[40,6400]{1,0:T(8,128)(2,1)S(1)} %collective-permute-done.7), channel_id=1, source_target_pairs={{1,0},{2,3},{5,4},{6,7},{9,8},{10,11},{13,12},{14,15},{17,16},{18,... | collective-permute-start | bytes 1536008 | tf_op jit(solution)/shard_map/ppermute | solution.py:96
  76.3 17.4 %copy-start.8 = (bf16[40,6400]{1,0:T(8,128)(2,1)}, bf16[40,6400]{1,0:T(8,128)(2,1)S(1)}, u32[]{:S(2)}) copy-start(bf16[40,6400]{1,0:T(8,128)(2,1)S(1)} %collective-permute-done.12) | copy-start | bytes 1536004
  76.3 17.3 %copy-start.9 = (bf16[40,6400]{1,0:T(8,128)(2,1)}, bf16[40,6400]{1,0:T(8,128)(2,1)S(1)}, u32[]{:S(2)}) copy-start(bf16[40,6400]{1,0:T(8,128)(2,1)S(1)} %collective-permute-done.11) | copy-start | bytes 1536004
  79.3 25.3 %collective-permute-start.16 = (bf16[2,40,3200]{2,1,0:T(8,128)(2,1)S(1)}, bf16[2,40,3200]{2,1,0:T(8,128)(2,1)S(1)}, u32[]{:S(2)}, u32[]{:S(2)}) collective-permute-start(bf16[2,40,3200]{2,1,0:T(8,128)(2,1)S(1)} %pad_maximum_fusion.2), channel_id=1, source_target_pairs={{0,16},{1,17},{2,18},{3,19},{4,20},{5,21},{6,22},{7,23},{8,24},{9,... | collective-permute-start | bytes 1536008 | tf_op jit(solution)/shard_map/ppermute | solution.py:96
  80.5 24.1 %collective-permute-start.17 = (bf16[2,40,3200]{2,1,0:T(8,128)(2,1)S(1)}, bf16[2,40,3200]{2,1,0:T(8,128)(2,1)S(1)}, u32[]{:S(2)}, u32[]{:S(2)}) collective-permute-start(bf16[2,40,3200]{2,1,0:T(8,128)(2,1)S(1)} %pad_maximum_fusion.3), channel_id=1, source_target_pairs={{0,8},{1,9},{2,10},{3,11},{4,12},{5,13},{6,14},{7,15},{8,0},{9,1},... | collective-permute-start | bytes 1536008 | tf_op jit(solution)/shard_map/ppermute | solution.py:96
  81.8 39.1 %collective-permute-start.18 = (bf16[40,6400]{1,0:T(8,128)(2,1)S(1)}, bf16[40,6400]{1,0:T(8,128)(2,1)S(1)}, u32[]{:S(2)}, u32[]{:S(2)}) collective-permute-start(bf16[40,6400]{1,0:T(8,128)(2,1)S(1)} %copy-done.18), channel_id=1, source_target_pairs={{3,0},{0,1},{5,2},{6,3},{1,4},{2,5},{7,6},{4,7},{11,8},{8,9},{13,1... | collective-permute-start | bytes 1536008 | tf_op jit(solution)/shard_map/ppermute | solution.py:96
  83.3 21.1 %collective-permute-start.15 = (bf16[40,6400]{1,0:T(8,128)(2,1)S(1)}, bf16[40,6400]{1,0:T(8,128)(2,1)S(1)}, u32[]{:S(2)}, u32[]{:S(2)}) collective-permute-start(bf16[40,6400]{1,0:T(8,128)(2,1)S(1)} %collective-permute-done.13), channel_id=1, source_target_pairs={{1,0},{2,3},{5,4},{6,7},{9,8},{10,11},{13,12},{14,15},{17,16},{18,... | collective-permute-start | bytes 1536008 | tf_op jit(solution)/shard_map/ppermute | solution.py:96
  84.6 57.3 %collective-permute-start.26 = (bf16[40,25600]{1,0:T(8,128)(2,1)}, bf16[40,25600]{1,0:T(8,128)(2,1)}, u32[]{:S(2)}, u32[]{:S(2)}) collective-permute-start(bf16[40,25600]{1,0:T(8,128)(2,1)} %pick.3.refs_0_), channel_id=1, source_target_pairs={{4,2},{5,3},{2,4},{3,5},{12,10},{13,11},{10,12},{11,13},{20,18},{2... | collective-permute-start | bytes 6144008 | tf_op jit(solution)/shard_map/ppermute | solution.py:96
  104.6 16.3 %copy-start = (bf16[2,40,6400]{2,1,0:T(8,128)(2,1)}, bf16[2,40,6400]{2,1,0:T(8,128)(2,1)S(1)}, u32[]{:S(2)}) copy-start(bf16[2,40,6400]{2,1,0:T(8,128)(2,1)S(1)} %pad_maximum_fusion.refs_6_.refs_10_.refs_2_.refs_7_) | copy-start | bytes 3072004
  104.6 20.0 %collective-permute-start.20 = (bf16[2,40,6400]{2,1,0:T(8,128)(2,1)S(1)}, bf16[2,40,6400]{2,1,0:T(8,128)(2,1)S(1)}, u32[]{:S(2)}, u32[]{:S(2)}) collective-permute-start(bf16[2,40,6400]{2,1,0:T(8,128)(2,1)S(1)} %pad_maximum_fusion.refs_6_.refs_10_.refs_2_.refs_7_), channel_id=1, source_target_pairs={{0,16},{1,17},{2,18},{3,19},{4,20},{5,21},{6,22},{7,23},{8,24},{9,... | collective-permute-start | bytes 3072008 | tf_op jit(solution)/shard_map/ppermute | solution.py:96
  104.9 25.7 %collective-permute-start.19 = (bf16[2,40,6400]{2,1,0:T(8,128)(2,1)S(1)}, bf16[2,40,6400]{2,1,0:T(8,128)(2,1)S(1)}, u32[]{:S(2)}, u32[]{:S(2)}) collective-permute-start(bf16[2,40,6400]{2,1,0:T(8,128)(2,1)S(1)} %pad_maximum_fusion.refs_6_.refs_10_.refs_2_.refs_7_), channel_id=1, source_target_pairs={{0,8},{1,9},{2,10},{3,11},{4,12},{5,13},{6,14},{7,15},{8,0},{9,1},... | collective-permute-start | bytes 3072008 | tf_op jit(solution)/shard_map/ppermute | solution.py:96
  106.5 25.0 %collective-permute-start.22 = (bf16[40,16000]{1,0:T(8,128)(2,1)}, bf16[40,16000]{1,0:T(8,128)(2,1)}, u32[]{:S(2)}, u32[]{:S(2)}) collective-permute-start(bf16[40,16000]{1,0:T(8,128)(2,1)} %collective-permute-done.5.refs_1_.refs_4_), channel_id=1, source_target_pairs={{0,4},{1,5},{2,6},{3,7},{4,0},{5,1},{6,2},{7,3},{8,12},{9,13},{10,... | collective-permute-start | bytes 3840008 | tf_op jit(solution)/shard_map/ppermute | solution.py:96
  120.9 10.6 %collective-permute-start.23 = (bf16[40,6400]{1,0:T(8,128)(2,1)S(1)}, bf16[40,6400]{1,0:T(8,128)(2,1)S(1)}, u32[]{:S(2)}, u32[]{:S(2)}) collective-permute-start(bf16[40,6400]{1,0:T(8,128)(2,1)S(1)} %collective-permute-done.18.refs_2_.refs_5_), channel_id=1, source_target_pairs={{0,4},{1,5},{2,6},{3,7},{4,0},{5,1},{6,2},{7,3},{8,12},{9,13},{10,... | collective-permute-start | bytes 1536008 | tf_op jit(solution)/shard_map/ppermute | solution.py:96
  124.6 17.2 %copy-start.1 = (bf16[2,40,6400]{2,1,0:T(8,128)(2,1)}, bf16[2,40,6400]{2,1,0:T(8,128)(2,1)S(1)}, u32[]{:S(2)}) copy-start(bf16[2,40,6400]{2,1,0:T(8,128)(2,1)S(1)} %collective-permute-done.20.refs_8_.refs_12_.refs_4_.refs_9_) | copy-start | bytes 3072004
  124.6 6.8 %collective-permute-start.21 = (bf16[40,3200]{1,0:T(8,128)(2,1)}, bf16[40,3200]{1,0:T(8,128)(2,1)S(1)}, u32[]{:S(2)}, u32[]{:S(2)}) collective-permute-start(bf16[40,3200]{1,0:T(8,128)(2,1)} %collective-permute-done.1.refs_0_.refs_3_), channel_id=1, source_target_pairs={{0,4},{1,5},{2,6},{3,7},{4,0},{5,1},{6,2},{7,3},{8,12},{9,13},{10,... | collective-permute-start | bytes 768008 | tf_op jit(solution)/shard_map/ppermute | solution.py:96
  132.2 13.5 %collective-permute-start.24 = (bf16[2,40,3200]{2,1,0:T(8,128)(2,1)}, bf16[2,40,3200]{2,1,0:T(8,128)(2,1)S(1)}, u32[]{:S(2)}, u32[]{:S(2)}) collective-permute-start(bf16[2,40,3200]{2,1,0:T(8,128)(2,1)} %slice.42), channel_id=1, source_target_pairs={{0,16},{1,17},{2,18},{3,19},{4,20},{5,21},{6,22},{7,23},{8,24},{9,... | collective-permute-start | bytes 1536008 | tf_op jit(solution)/shard_map/ppermute | solution.py:96
  132.4 13.2 %collective-permute-start.25 = (bf16[2,40,3200]{2,1,0:T(8,128)(2,1)}, bf16[2,40,3200]{2,1,0:T(8,128)(2,1)S(1)}, u32[]{:S(2)}, u32[]{:S(2)}) collective-permute-start(bf16[2,40,3200]{2,1,0:T(8,128)(2,1)} %slice.43), channel_id=1, source_target_pairs={{0,8},{1,9},{2,10},{3,11},{4,12},{5,13},{6,14},{7,15},{8,0},{9,1},... | collective-permute-start | bytes 1536008 | tf_op jit(solution)/shard_map/ppermute | solution.py:96
  145.7 9.6 %collective-permute-start.27 = (bf16[40,25600]{1,0:T(8,128)(2,1)}, bf16[40,25600]{1,0:T(8,128)(2,1)}, u32[]{:S(2)}, u32[]{:S(2)}) collective-permute-start(bf16[40,25600]{1,0:T(8,128)(2,1)} %collective-permute-done.26.refs_4_), channel_id=1, source_target_pairs={{0,4},{1,5},{2,6},{3,7},{4,0},{5,1},{6,2},{7,3},{8,12},{9,13},{10,... | collective-permute-start | bytes 6144008 | tf_op jit(solution)/shard_map/ppermute | solution.py:96
  185.0 3.0 %collective-permute-start.28 = (bf16[40,10240]{1,0:T(8,128)(2,1)}, bf16[40,10240]{1,0:T(8,128)(2,1)S(1)}, u32[]{:S(2)}, u32[]{:S(2)}) collective-permute-start(bf16[40,10240]{1,0:T(8,128)(2,1)} %get-tuple-element.135), channel_id=1, source_target_pairs={{0,4},{1,5},{2,6},{3,7},{4,0},{5,1},{6,2},{7,3},{8,12},{9,13},{10,... | collective-permute-start | bytes 2457608 | tf_op jit(solution)/shard_map/ppermute | solution.py:96
  185.8 16.7 %collective-permute-start.30 = (bf16[40,15360]{1,0:T(8,128)(2,1)}, bf16[40,15360]{1,0:T(8,128)(2,1)S(1)}, u32[]{:S(2)}, u32[]{:S(2)}) collective-permute-start(bf16[40,15360]{1,0:T(8,128)(2,1)} %get-tuple-element.137), channel_id=1, source_target_pairs={{0,4},{1,5},{2,6},{3,7},{4,0},{5,1},{6,2},{7,3},{8,12},{9,13},{10,... | collective-permute-start | bytes 3686408 | tf_op jit(solution)/shard_map/ppermute | solution.py:96
  190.2 21.7 %collective-permute-start.29 = (bf16[40,10240]{1,0:T(8,128)(2,1)}, bf16[40,10240]{1,0:T(8,128)(2,1)}, u32[]{:S(2)}, u32[]{:S(2)}) collective-permute-start(bf16[40,10240]{1,0:T(8,128)(2,1)} %add_convert_fusion.1), channel_id=1, source_target_pairs={{0,3},{1,0},{2,5},{3,6},{4,1},{5,2},{6,7},{7,4},{8,11},{9,8},{10,1... | collective-permute-start | bytes 2457608 | tf_op jit(solution)/shard_map/ppermute | solution.py:96
  197.8 21.6 %collective-permute-start.34 = (bf16[40,6400]{1,0:T(8,128)(2,1)}, bf16[40,6400]{1,0:T(8,128)(2,1)}, u32[]{:S(2)}, u32[]{:S(2)}) collective-permute-start(bf16[40,6400]{1,0:T(8,128)(2,1)} %get-tuple-element.147), channel_id=1, source_target_pairs={{0,4},{1,5},{2,6},{3,7},{4,0},{5,1},{6,2},{7,3},{8,12},{9,13},{10,... | collective-permute-start | bytes 1536008 | tf_op jit(solution)/shard_map/ppermute | solution.py:96
  201.9 22.0 %collective-permute-start.36 = (bf16[40,6400]{1,0:T(8,128)(2,1)}, bf16[40,6400]{1,0:T(8,128)(2,1)}, u32[]{:S(2)}, u32[]{:S(2)}) collective-permute-start(bf16[40,6400]{1,0:T(8,128)(2,1)} %get-tuple-element.149), channel_id=1, source_target_pairs={{0,4},{1,5},{2,6},{3,7},{4,0},{5,1},{6,2},{7,3},{8,12},{9,13},{10,... | collective-permute-start | bytes 1536008 | tf_op jit(solution)/shard_map/ppermute | solution.py:96
  202.0 28.2 %collective-permute-start.38 = (bf16[40,6400]{1,0:T(8,128)(2,1)}, bf16[40,6400]{1,0:T(8,128)(2,1)}, u32[]{:S(2)}, u32[]{:S(2)}) collective-permute-start(bf16[40,6400]{1,0:T(8,128)(2,1)} %get-tuple-element.151), channel_id=1, source_target_pairs={{0,4},{1,5},{2,6},{3,7},{4,0},{5,1},{6,2},{7,3},{8,12},{9,13},{10,... | collective-permute-start | bytes 1536008 | tf_op jit(solution)/shard_map/ppermute | solution.py:96
  202.4 32.0 %collective-permute-start.32 = (bf16[40,6400]{1,0:T(8,128)(2,1)}, bf16[40,6400]{1,0:T(8,128)(2,1)}, u32[]{:S(2)}, u32[]{:S(2)}) collective-permute-start(bf16[40,6400]{1,0:T(8,128)(2,1)} %get-tuple-element.142), channel_id=1, source_target_pairs={{0,4},{1,5},{2,6},{3,7},{4,0},{5,1},{6,2},{7,3},{8,12},{9,13},{10,... | collective-permute-start | bytes 1536008 | tf_op jit(solution)/shard_map/ppermute | solution.py:96
  211.9 30.6 %collective-permute-start.31 = (bf16[40,15360]{1,0:T(8,128)(2,1)S(1)}, bf16[40,15360]{1,0:T(8,128)(2,1)}, u32[]{:S(2)}, u32[]{:S(2)}) collective-permute-start(bf16[40,15360]{1,0:T(8,128)(2,1)S(1)} %add_convert_fusion), channel_id=1, source_target_pairs={{0,3},{1,0},{2,5},{3,6},{4,1},{5,2},{6,7},{7,4},{8,11},{9,8},{10,1... | collective-permute-start | bytes 3686408 | tf_op jit(solution)/shard_map/ppermute | solution.py:96
  221.6 45.8 %collective-permute-start.35 = (bf16[40,6400]{1,0:T(8,128)(2,1)}, bf16[40,6400]{1,0:T(8,128)(2,1)}, u32[]{:S(2)}, u32[]{:S(2)}) collective-permute-start(bf16[40,6400]{1,0:T(8,128)(2,1)} %add_convert_fusion.4.refs_2_), channel_id=1, source_target_pairs={{2,4},{3,5},{4,2},{5,3},{10,12},{11,13},{12,10},{13,11},{18,20},{1... | collective-permute-start | bytes 1536008 | tf_op jit(solution)/shard_map/ppermute | solution.py:96
  226.0 46.9 %collective-permute-start.37 = (bf16[40,6400]{1,0:T(8,128)(2,1)}, bf16[40,6400]{1,0:T(8,128)(2,1)}, u32[]{:S(2)}, u32[]{:S(2)}) collective-permute-start(bf16[40,6400]{1,0:T(8,128)(2,1)} %add_convert_fusion.3.refs_3_), channel_id=1, source_target_pairs={{2,4},{3,5},{4,2},{5,3},{10,12},{11,13},{12,10},{13,11},{18,20},{1... | collective-permute-start | bytes 1536008 | tf_op jit(solution)/shard_map/ppermute | solution.py:96
  232.2 46.2 %collective-permute-start.39 = (bf16[40,6400]{1,0:T(8,128)(2,1)}, bf16[40,6400]{1,0:T(8,128)(2,1)}, u32[]{:S(2)}, u32[]{:S(2)}) collective-permute-start(bf16[40,6400]{1,0:T(8,128)(2,1)} %add_convert_fusion.2.refs_4_), channel_id=1, source_target_pairs={{2,4},{3,5},{4,2},{5,3},{10,12},{11,13},{12,10},{13,11},{18,20},{1... | collective-permute-start | bytes 1536008 | tf_op jit(solution)/shard_map/ppermute | solution.py:96
  236.4 47.4 %collective-permute-start.33 = (bf16[40,6400]{1,0:T(8,128)(2,1)}, bf16[40,6400]{1,0:T(8,128)(2,1)}, u32[]{:S(2)}, u32[]{:S(2)}) collective-permute-start(bf16[40,6400]{1,0:T(8,128)(2,1)} %add_convert_fusion.5.refs_1_), channel_id=1, source_target_pairs={{2,4},{3,5},{4,2},{5,3},{10,12},{11,13},{12,10},{13,11},{18,20},{1... | collective-permute-start | bytes 1536008 | tf_op jit(solution)/shard_map/ppermute | solution.py:96
  (11 other events, 93.6 us)

commit v2 on v1

--- a/solution.py
+++ b/solution.py
@@ -271,10 +271,10 @@
                 y = (i * step + j) * quad + r
                 put_both(turned, pl.ds(y, planes, stride=turned_pitch), along_z[j * planes : (j + 1) * planes])
 
-    @pl.loop(0, planes // 20)
+    @pl.loop(0, planes // 40)
     def _(i):
-        for j in range(20):
-            x = i * 20 + j
+        for j in range(40):
+            x = i * 40 + j
             along_z = both(turned, pl.ds(x * turned_pitch, extent)).astype(jnp.bfloat16)
             put_both(out, pl.ds(x, extent, stride=plane_pitch), dot(cas[...], along_z))
 
@@ -283,7 +283,7 @@
     extent = square.shape[0]
     planes = extent // ring
     strength = (extent * spacing) ** 2 / math.pi
-    rows = 32
+    rows = 40
 
     @pl.loop(0, extent // rows)
     def _(step):
@@ -307,10 +307,10 @@
     planes, points = source.shape
     extent = cas.shape[0]
 
-    @pl.loop(0, planes // 20)
+    @pl.loop(0, planes // 40)
     def _(i):
-        for j in range(20):
-            x = i * 20 + j
+        for j in range(40):
+            x = i * 40 + j
             column_x = both(back_x, pl.ds(x, extent, stride=plane_pitch)).astype(jnp.bfloat16)
             put_both(turned, pl.ds(x * turned_pitch, extent), dot(cas[...], column_x))
 

time: 288 us -> 288 us (level)
  transfers between devices with their start and end apart: 40 -> 40, of which waited for: 18 -> 18; matrix products, arithmetic and copies ran while one was open for 9% -> 9% of each run, Pallas kernels for 18% -> 17%
where the time goes in v2:
time: 288 us; the launch traced here: 287 us
  waiting for transfers between devices  104 us (36%)
  Pallas kernels  88 us (31%)
  starting transfers between devices  66.2 us (23%)
  other arithmetic  15.7 us (5%)
  local copies, waits for them, and re-layouts  10.3 us (4%)
  between operations  3.35 us (1%)
    ppermute x40, waiting for transfers between devices, move(): lax.ppermute(x, ('band', 'grid'), [(place(*a), place(*b)) for a, b in rou...  104 us
    ppermute x40, starting transfers between devices, move(): lax.ppermute(x, ('band', 'grid'), [(place(*a), place(*b)) for a, b in rou...  66.2 us
    pallas_call x1, Pallas kernels, central(): pl.pallas_call(functools.partial(central_kernel, home, direct), out_shape...  30 us
    pallas_call x3, Pallas kernels, forward(): pl.pallas_call(functools.partial(forward_kernel, place, first, len(target...  24.9 us
    pallas_call x2, Pallas kernels, backward(): pl.pallas_call(functools.partial(backward_kernel, places, first, parts),...  14.7 us
    convert_element_type x6, other arithmetic, add(): return (a.astype(jnp.float32) + b.astype(jnp.float32)).astype(jnp.bfloat16)  10.7 us
    pallas_call x2, Pallas kernels, pick(): pl.pallas_call(functools.partial(pick_kernel, which), out_shape=[jax.Shap...  8.5 us
    pallas_call x2, Pallas kernels, put(): pl.pallas_call(functools.partial(put_kernel, len(choices), len(before)),...  6.33 us
  transfers between devices with their start and end apart: 40, of which 18 were waited for; matrix products, arithmetic and copies ran while one was open for 9% of the time, Pallas kernels for 17%

profile of v2, /device:TPU:1, one launch (start us, length us, event | category | flops | bytes accessed | tf_op | source)
XLA Modules:
  0.0 287.2 jit_solution(3637203398604791788)
XLA Ops:
  0.0 4.8 %pick.2 = (bf16[40,25600]{1,0:T(8,128)(2,1)}, bf16[40,3200]{1,0:T(8,128)(2,1)}, bf16[40,16000]{1,0:T(8,128)(2,1)}, bf16[40,6400]{1,0:T(8,128)(2,1)}) custom-call(s32[2]{0:T(128)} %source_index.5, bf16[2,40,25600]{2,1,0:T(8,128)(2,1)} %orbitals.4), custom_call_target="tpu_custom_call" | custom-call | flops 1000000 | bytes 10000 | tf_op jit(solution)/shard_map/pick/pallas_call | solution.py:419
  4.9 4.8 %collective-permute-start.1 = (bf16[40,3200]{1,0:T(8,128)(2,1)}, bf16[40,3200]{1,0:T(8,128)(2,1)}, u32[]{:S(2)}, u32[]{:S(2)}) collective-permute-start(bf16[40,3200]{1,0:T(8,128)(2,1)} %get-tuple-element.86), channel_id=1, source_target_pairs={{3,0},{0,1},{5,2},{6,3},{1,4},{2,5},{7,6},{4,7},{11,8},{8,9},{13,1... | collective-permute-start | bytes 768008 | tf_op jit(solution)/shard_map/ppermute | solution.py:96
  9.7 3.5 %cut.1 = (bf16[40,6400]{1,0:T(8,128)(2,1)}, bf16[40,6400]{1,0:T(8,128)(2,1)}, bf16[40,6400]{1,0:T(8,128)(2,1)}, bf16[40,6400]{1,0:T(8,128)(2,1)}) custom-call(s32[2]{0:T(128)} %source_index.5, bf16[2,40,25600]{2,1,0:T(8,128)(2,1)} %orbitals.4, bf16[40,25600]{1,0:T(8,128)(2,1)} %collective-permute-done.crossed), custom_call_target="tpu_custom_call" | custom-call | flops 1000000 | bytes 10000 | tf_op jit(solution)/shard_map/cut/pallas_call | solution.py:433
  14.5 3.7 %collective-permute-start.5 = (bf16[40,16000]{1,0:T(8,128)(2,1)}, bf16[40,16000]{1,0:T(8,128)(2,1)}, u32[]{:S(2)}, u32[]{:S(2)}) collective-permute-start(bf16[40,16000]{1,0:T(8,128)(2,1)} %get-tuple-element.94), channel_id=1, source_target_pairs={{3,0},{0,1},{5,2},{6,3},{1,4},{2,5},{7,6},{4,7},{11,8},{8,9},{13,1... | collective-permute-start | bytes 3840008 | tf_op jit(solution)/shard_map/ppermute | solution.py:96
  21.9 1.3 dynamic_slice.3
  28.2 1.5 multiply_convert_fusion
  29.8 3.7 %pick.3.refs_0_ = bf16[40,25600]{1,0:T(8,128)(2,1)} custom-call(s32[2]{0:T(128)} %source_index.5, bf16[2,40,25600]{2,1,0:T(8,128)(2,1)} %orbitals.4), custom_call_target="tpu_custom_call" | custom-call | flops 1000000 | bytes 10000 | tf_op jit(solution)/shard_map/pick/pallas_call | solution.py:419
  33.5 11.0 %collective-permute-done.3 = bf16[40,6400]{1,0:T(8,128)(2,1)S(1)} collective-permute-done((bf16[40,6400]{1,0:T(8,128)(2,1)}, bf16[40,6400]{1,0:T(8,128)(2,1)S(1)}, u32[]{:S(2)}, u32[]{:S(2)}) %collective-permute-start.3) | collective-permute-done | bytes 512032 | tf_op jit(solution)/shard_map/ppermute | solution.py:96
  45.8 1.9 collective-permute-start.10
  47.8 1.3 collective-permute-start.9
  51.1 1.3 collective-permute-start.6
  55.6 5.6 %collective-permute-done.9 = bf16[40,6400]{1,0:T(8,128)(2,1)S(1)} collective-permute-done((bf16[40,6400]{1,0:T(8,128)(2,1)S(1)}, bf16[40,6400]{1,0:T(8,128)(2,1)S(1)}, u32[]{:S(2)}, u32[]{:S(2)}) %collective-permute-start.9) | collective-permute-done | bytes 512032 | tf_op jit(solution)/shard_map/ppermute | solution.py:96
  62.1 1.6 collective-permute-done.6
  65.0 1.3 collective-permute-start.14
  66.4 9.9 %collective-permute-done.12 = bf16[40,6400]{1,0:T(8,128)(2,1)S(1)} collective-permute-done((bf16[40,6400]{1,0:T(8,128)(2,1)S(1)}, bf16[40,6400]{1,0:T(8,128)(2,1)S(1)}, u32[]{:S(2)}, u32[]{:S(2)}) %collective-permute-start.12) | collective-permute-done | bytes 512032 | tf_op jit(solution)/shard_map/ppermute | solution.py:96
  76.5 2.8 collective-permute-done.14
  81.8 1.5 collective-permute-start.18
  83.3 1.3 collective-permute-start.15
  84.6 8.8 %collective-permute-start.26 = (bf16[40,25600]{1,0:T(8,128)(2,1)}, bf16[40,25600]{1,0:T(8,128)(2,1)}, u32[]{:S(2)}, u32[]{:S(2)}) collective-permute-start(bf16[40,25600]{1,0:T(8,128)(2,1)} %pick.3.refs_0_), channel_id=1, source_target_pairs={{4,2},{5,3},{2,4},{3,5},{12,10},{13,11},{10,12},{11,13},{20,18},{2... | collective-permute-start | bytes 6144008 | tf_op jit(solution)/shard_map/ppermute | solution.py:96
  93.5 10.9 %collective-permute-done.15 = bf16[40,6400]{1,0:T(8,128)(2,1)S(1)} collective-permute-done((bf16[40,6400]{1,0:T(8,128)(2,1)S(1)}, bf16[40,6400]{1,0:T(8,128)(2,1)S(1)}, u32[]{:S(2)}, u32[]{:S(2)}) %collective-permute-start.15) | collective-permute-done | bytes 512032 | tf_op jit(solution)/shard_map/ppermute | solution.py:96
  106.5 5.1 %collective-permute-start.22 = (bf16[40,16000]{1,0:T(8,128)(2,1)}, bf16[40,16000]{1,0:T(8,128)(2,1)}, u32[]{:S(2)}, u32[]{:S(2)}) collective-permute-start(bf16[40,16000]{1,0:T(8,128)(2,1)} %collective-permute-done.5.refs_1_.refs_4_), channel_id=1, source_target_pairs={{0,4},{1,5},{2,6},{3,7},{4,0},{5,1},{6,2},{7,3},{8,12},{9,13},{10,... | collective-permute-start | bytes 3840008 | tf_op jit(solution)/shard_map/ppermute | solution.py:96
  112.4 8.2 %forward.3.refs_0_ = f32[2,6560,128]{2,1,0:T(8,128)} custom-call(s32[6]{0:T(128)} %stack.100.flags, bf16[40,25600]{1,0:T(8,128)(2,1)} %pick.3.refs_0_, bf16[40,25600]{1,0:T(8,128)(2,1)} %collective-permute-done.10.refs_1_, bf16[1,40,6400]{2,1,0:T(8,128)(2,1)} %bitcast.37, bf16[1,40,6400]{2,1,0:T(8,128)(2,1)} %bitcast.43, bf16[1,40,6400]{2,1,0:T(8,128)(2,1)} %bitcast.40, ...), custom_call_target="tpu_custom_call" | custom-call | flops 1000000 | bytes 10000 | tf_op jit(solution)/shard_map/forward/pallas_call | solution.py:471
  120.8 3.9 %collective-permute-done.20.refs_8_.refs_12_.refs_4_.refs_9_ = bf16[2,40,6400]{2,1,0:T(8,128)(2,1)S(1)} collective-permute-done((bf16[2,40,6400]{2,1,0:T(8,128)(2,1)S(1)}, bf16[2,40,6400]{2,1,0:T(8,128)(2,1)S(1)}, u32[]{:S(2)}, u32[]{:S(2)}) %collective-permute-start.20) | collective-permute-done | bytes 1024032 | tf_op jit(solution)/shard_map/ppermute | solution.py:96
  124.6 5.1 %collective-permute-start.21 = (bf16[40,3200]{1,0:T(8,128)(2,1)}, bf16[40,3200]{1,0:T(8,128)(2,1)S(1)}, u32[]{:S(2)}, u32[]{:S(2)}) collective-permute-start(bf16[40,3200]{1,0:T(8,128)(2,1)} %collective-permute-done.1.refs_0_.refs_3_), channel_id=1, source_target_pairs={{0,4},{1,5},{2,6},{3,7},{4,0},{5,1},{6,2},{7,3},{8,12},{9,13},{10,... | collective-permute-start | bytes 768008 | tf_op jit(solution)/shard_map/ppermute | solution.py:96
  133.3 8.4 %forward.4.refs_1_ = f32[2,6560,128]{2,1,0:T(8,128)} custom-call(s32[6]{0:T(128)} %stack.100.flags, bf16[40,3200]{1,0:T(8,128)(2,1)} %collective-permute-done.1.refs_0_.refs_3_, bf16[40,16000]{1,0:T(8,128)(2,1)} %collective-permute-done.5.refs_1_.refs_4_, bf16[40,6400]{1,0:T(8,128)(2,1)} %copy-done.10, bf16[40,3200]{1,0:T(8,128)(2,1)} %copy-done.14, ...), custom_call_target="tpu_custom_call" | custom-call | flops 1000000 | bytes 10000 | tf_op jit(solution)/shard_map/forward/pallas_call | solution.py:471
  141.7 4.0 %collective-permute-done.24.refs_9_.refs_13_.refs_5_.refs_10_ = bf16[2,40,3200]{2,1,0:T(8,128)(2,1)S(1)} collective-permute-done((bf16[2,40,3200]{2,1,0:T(8,128)(2,1)}, bf16[2,40,3200]{2,1,0:T(8,128)(2,1)S(1)}, u32[]{:S(2)}, u32[]{:S(2)}) %collective-permute-start.24) | collective-permute-done | bytes 512032 | tf_op jit(solution)/shard_map/ppermute | solution.py:96
  146.7 8.3 %forward.5.refs_2_ = f32[2,6560,128]{2,1,0:T(8,128)} custom-call(s32[6]{0:T(128)} %stack.100.flags, bf16[40,3200]{1,0:T(8,128)(2,1)} %copy-done.14, bf16[40,16000]{1,0:T(8,128)(2,1)} %collective-permute-done.22.refs_4_.refs_1_, bf16[40,6400]{1,0:T(8,128)(2,1)} %copy-done.11, bf16[40,3200]{1,0:T(8,128)(2,1)} %collective-permute-done.1.refs_0_.refs_3_, ...), custom_call_target="tpu_custom_call" | custom-call | flops 1000000 | bytes 10000 | tf_op jit(solution)/shard_map/forward/pallas_call | solution.py:471
  155.1 30.0 %central.1 = (bf16[40,10240]{1,0:T(8,128)(2,1)}, bf16[40,15360]{1,0:T(8,128)(2,1)}, bf16[40,10240]{1,0:T(8,128)(2,1)}, bf16[40,15360]{1,0:T(8,128)(2,1)}, f32[2,...) custom-call(s32[6]{0:T(128)} %stack.100.flags, f32[2,6560,128]{2,1,0:T(8,128)} %forward.3.refs_0_, ...), custom_call_target="tpu_custom_call" | custom-call | flops 1000000 | bytes 10000 | tf_op jit(solution)/shard_map/central/pallas_call | solution.py:495
  186.0 2.1 collective-permute-done.28
  188.1 2.2 add_convert_fusion.1
  190.3 7.4 %backward.2 = (bf16[40,6400]{1,0:T(8,128)(2,1)}, bf16[40,6400]{1,0:T(8,128)(2,1)}, bf16[40,6400]{1,0:T(8,128)(2,1)}, bf16[40,6400]{1,0:T(8,128)(2,1)}) custom-call(s32[6]{0:T(128)} %stack.100.flags, f32[2,6560,128]{2,1,0:T(8,128)} %get-tuple-element.144.refs_0_.refs_1_, f32[2,6560,128]{2,1,0:T(8,128)} %get-tuple-element.143.refs_1_.refs_0_, ...), custom_call_target="tpu_custom_call" | custom-call | flops 1000000 | bytes 10000 | tf_op jit(solution)/shard_map/backward/pallas_call | solution.py:520
  197.7 4.1 %collective-permute-start.34 = (bf16[40,6400]{1,0:T(8,128)(2,1)}, bf16[40,6400]{1,0:T(8,128)(2,1)}, u32[]{:S(2)}, u32[]{:S(2)}) collective-permute-start(bf16[40,6400]{1,0:T(8,128)(2,1)} %get-tuple-element.147), channel_id=1, source_target_pairs={{0,4},{1,5},{2,6},{3,7},{4,0},{5,1},{6,2},{7,3},{8,12},{9,13},{10,... | collective-permute-start | bytes 1536008 | tf_op jit(solution)/shard_map/ppermute | solution.py:96
  202.7 9.3 %collective-permute-done.29.refs_0_ = bf16[40,10240]{1,0:T(8,128)(2,1)} collective-permute-done((bf16[40,10240]{1,0:T(8,128)(2,1)}, bf16[40,10240]{1,0:T(8,128)(2,1)}, u32[]{:S(2)}, u32[]{:S(2)}) %collective-permute-start.29) | collective-permute-done | bytes 819232 | tf_op jit(solution)/shard_map/ppermute | solution.py:96
  212.0 7.3 %backward.3 = (bf16[40,6400]{1,0:T(8,128)(2,1)}, bf16[40,6400]{1,0:T(8,128)(2,1)}, bf16[40,6400]{1,0:T(8,128)(2,1)}, bf16[40,6400]{1,0:T(8,128)(2,1)}) custom-call(s32[6]{0:T(128)} %stack.100.flags, f32[2,6560,128]{2,1,0:T(8,128)} %get-tuple-element.143.refs_1_.refs_0_, f32[2,6560,128]{2,1,0:T(8,128)} %get-tuple-element.144.refs_0_.refs_1_, ...), custom_call_target="tpu_custom_call" | custom-call | flops 1000000 | bytes 10000 | tf_op jit(solution)/shard_map/backward/pallas_call | solution.py:520
  219.4 2.2 add_convert_fusion.4.refs_2_
  221.6 2.3 collective-permute-start.35
  223.8 2.1 add_convert_fusion.3.refs_3_
  225.9 4.2 %collective-permute-start.37 = (bf16[40,6400]{1,0:T(8,128)(2,1)}, bf16[40,6400]{1,0:T(8,128)(2,1)}, u32[]{:S(2)}, u32[]{:S(2)}) collective-permute-start(bf16[40,6400]{1,0:T(8,128)(2,1)} %add_convert_fusion.3.refs_3_), channel_id=1, source_target_pairs={{2,4},{3,5},{4,2},{5,3},{10,12},{11,13},{12,10},{13,11},{18,20},{1... | collective-permute-start | bytes 1536008 | tf_op jit(solution)/shard_map/ppermute | solution.py:96
  230.1 2.0 add_convert_fusion.2.refs_4_
  232.1 2.3 collective-permute-start.39
  234.4 2.0 add_convert_fusion.5.refs_1_
  236.4 4.2 %collective-permute-start.33 = (bf16[40,6400]{1,0:T(8,128)(2,1)}, bf16[40,6400]{1,0:T(8,128)(2,1)}, u32[]{:S(2)}, u32[]{:S(2)}) collective-permute-start(bf16[40,6400]{1,0:T(8,128)(2,1)} %add_convert_fusion.5.refs_1_), channel_id=1, source_target_pairs={{2,4},{3,5},{4,2},{5,3},{10,12},{11,13},{12,10},{13,11},{18,20},{1... | collective-permute-start | bytes 1536008 | tf_op jit(solution)/shard_map/ppermute | solution.py:96
  242.6 3.3 %put.2.refs_0_ = bf16[2,40,25600]{2,1,0:T(8,128)(2,1)} custom-call(s32[2]{0:T(128)} %pad_add_fusion.1.flags, bf16[40,10240]{1,0:T(8,128)(2,1)} %collective-permute-done.29.refs_0_, bf16[40,15360]{1,0:T(8,128)(2,1)} %collective-permute-done.31.refs_1_), custom_call_target="tpu_custom_call" | custom-call | flops 1000000 | bytes 10000 | tf_op jit(solution)/shard_map/put/pallas_call | solution.py:450
  245.9 21.6 %collective-permute-done.35.refs_6_ = bf16[40,6400]{1,0:T(8,128)(2,1)} collective-permute-done((bf16[40,6400]{1,0:T(8,128)(2,1)}, bf16[40,6400]{1,0:T(8,128)(2,1)}, u32[]{:S(2)}, u32[]{:S(2)}) %collective-permute-start.35) | collective-permute-done | bytes 512032 | tf_op jit(solution)/shard_map/ppermute | solution.py:96
  267.5 5.5 %collective-permute-done.37.refs_7_ = bf16[40,6400]{1,0:T(8,128)(2,1)} collective-permute-done((bf16[40,6400]{1,0:T(8,128)(2,1)}, bf16[40,6400]{1,0:T(8,128)(2,1)}, u32[]{:S(2)}, u32[]{:S(2)}) %collective-permute-start.37) | collective-permute-done | bytes 512032 | tf_op jit(solution)/shard_map/ppermute | solution.py:96
  273.0 5.5 %collective-permute-done.39.refs_8_ = bf16[40,6400]{1,0:T(8,128)(2,1)} collective-permute-done((bf16[40,6400]{1,0:T(8,128)(2,1)}, bf16[40,6400]{1,0:T(8,128)(2,1)}, u32[]{:S(2)}, u32[]{:S(2)}) %collective-permute-start.39) | collective-permute-done | bytes 512032 | tf_op jit(solution)/shard_map/ppermute | solution.py:96
  278.5 5.5 %collective-permute-done.33.refs_5_ = bf16[40,6400]{1,0:T(8,128)(2,1)} collective-permute-done((bf16[40,6400]{1,0:T(8,128)(2,1)}, bf16[40,6400]{1,0:T(8,128)(2,1)}, u32[]{:S(2)}, u32[]{:S(2)}) %collective-permute-start.33) | collective-permute-done | bytes 512032 | tf_op jit(solution)/shard_map/ppermute | solution.py:96
  284.0 3.1 %put.3 = bf16[2,40,25600]{2,1,0:T(8,128)(2,1)} custom-call(s32[2]{0:T(128)} %pad_add_fusion.flags, bf16[2,40,25600]{2,1,0:T(8,128)(2,1)} %put.2.refs_0_, bf16[40,6400]{1,0:T(8,128)(2,1)} %add_convert_fusion.5.refs_1_, bf16[40,6400]{1,0:T(8,128)(2,1)} %add_convert_fusion.4.refs_2_, ...), custom_call_target="tpu_custom_call", output_to_operand_aliasing={{}: (1, {})} | custom-call | flops 1000000 | bytes 10000 | tf_op jit(solution)/shard_map/put/pallas_call | solution.py:450
  (118 shorter events, 30.3 us)
Async XLA Ops:
  4.8 4.9 %collective-permute-start = (bf16[40,25600]{1,0:T(8,128)(2,1)}, bf16[40,25600]{1,0:T(8,128)(2,1)}, u32[]{:S(2)}, u32[]{:S(2)}) collective-permute-start(bf16[40,25600]{1,0:T(8,128)(2,1)} %get-tuple-element.81), channel_id=1, source_target_pairs={{0,4},{1,5},{2,6},{3,7},{4,0},{5,1},{6,2},{7,3},{8,12},{9,13},{10,... | collective-permute-start | bytes 6144008 | tf_op jit(solution)/shard_map/ppermute | solution.py:96
  4.9 9.6 %collective-permute-start.1 = (bf16[40,3200]{1,0:T(8,128)(2,1)}, bf16[40,3200]{1,0:T(8,128)(2,1)}, u32[]{:S(2)}, u32[]{:S(2)}) collective-permute-start(bf16[40,3200]{1,0:T(8,128)(2,1)} %get-tuple-element.86), channel_id=1, source_target_pairs={{3,0},{0,1},{5,2},{6,3},{1,4},{2,5},{7,6},{4,7},{11,8},{8,9},{13,1... | collective-permute-start | bytes 768008 | tf_op jit(solution)/shard_map/ppermute | solution.py:96
  14.5 31.2 %collective-permute-start.5 = (bf16[40,16000]{1,0:T(8,128)(2,1)}, bf16[40,16000]{1,0:T(8,128)(2,1)}, u32[]{:S(2)}, u32[]{:S(2)}) collective-permute-start(bf16[40,16000]{1,0:T(8,128)(2,1)} %get-tuple-element.94), channel_id=1, source_target_pairs={{3,0},{0,1},{5,2},{6,3},{1,4},{2,5},{7,6},{4,7},{11,8},{8,9},{13,1... | collective-permute-start | bytes 3840008 | tf_op jit(solution)/shard_map/ppermute | solution.py:96
  18.4 15.1 %collective-permute-start.2 = (bf16[40,6400]{1,0:T(8,128)(2,1)}, bf16[40,6400]{1,0:T(8,128)(2,1)S(1)}, u32[]{:S(2)}, u32[]{:S(2)}) collective-permute-start(bf16[40,6400]{1,0:T(8,128)(2,1)} %get-tuple-element.90), channel_id=1, source_target_pairs={{0,8},{1,9},{2,10},{3,11},{4,12},{5,13},{6,14},{7,15},{8,0},{9,1},... | collective-permute-start | bytes 1536008 | tf_op jit(solution)/shard_map/ppermute | solution.py:96
  19.7 24.8 %collective-permute-start.3 = (bf16[40,6400]{1,0:T(8,128)(2,1)}, bf16[40,6400]{1,0:T(8,128)(2,1)S(1)}, u32[]{:S(2)}, u32[]{:S(2)}) collective-permute-start(bf16[40,6400]{1,0:T(8,128)(2,1)} %get-tuple-element.91), channel_id=1, source_target_pairs={{0,16},{1,17},{2,18},{3,19},{4,20},{5,21},{6,22},{7,23},{8,24},{9,... | collective-permute-start | bytes 1536008 | tf_op jit(solution)/shard_map/ppermute | solution.py:96
  20.9 23.6 %collective-permute-start.4 = (bf16[40,6400]{1,0:T(8,128)(2,1)}, bf16[40,6400]{1,0:T(8,128)(2,1)S(1)}, u32[]{:S(2)}, u32[]{:S(2)}) collective-permute-start(bf16[40,6400]{1,0:T(8,128)(2,1)} %get-tuple-element.92), channel_id=1, source_target_pairs={{0,24},{1,25},{2,26},{3,27},{4,28},{5,29},{6,30},{7,31},{8,16},{9,... | collective-permute-start | bytes 1536008 | tf_op jit(solution)/shard_map/ppermute | solution.py:96
  29.8 17.9 %copy-start.17 = (bf16[40,6400]{1,0:T(8,128)(2,1)S(1)}, bf16[40,6400]{1,0:T(8,128)(2,1)}, u32[]{:S(2)}) copy-start(bf16[40,6400]{1,0:T(8,128)(2,1)} %get-tuple-element.96) | copy-start | bytes 1536004
  45.8 18.0 %collective-permute-start.10 = (bf16[40,25600]{1,0:T(8,128)(2,1)}, bf16[40,25600]{1,0:T(8,128)(2,1)}, u32[]{:S(2)}, u32[]{:S(2)}) collective-permute-start(bf16[40,25600]{1,0:T(8,128)(2,1)} %pick.3.refs_0_), channel_id=1, source_target_pairs={{0,4},{1,5},{2,6},{3,7},{4,0},{5,1},{6,2},{7,3},{8,12},{9,13},{10,... | collective-permute-start | bytes 6144008 | tf_op jit(solution)/shard_map/ppermute | solution.py:96
  47.8 28.6 %copy-start.3 = (bf16[40,6400]{1,0:T(8,128)(2,1)}, bf16[40,6400]{1,0:T(8,128)(2,1)S(1)}, u32[]{:S(2)}) copy-start(bf16[40,6400]{1,0:T(8,128)(2,1)S(1)} %select_select_fusion) | copy-start | bytes 1536004
  47.8 13.4 %collective-permute-start.9 = (bf16[40,6400]{1,0:T(8,128)(2,1)S(1)}, bf16[40,6400]{1,0:T(8,128)(2,1)S(1)}, u32[]{:S(2)}, u32[]{:S(2)}) collective-permute-start(bf16[40,6400]{1,0:T(8,128)(2,1)S(1)} %select_select_fusion), channel_id=1, source_target_pairs={{0,16},{1,17},{2,18},{3,19},{4,20},{5,21},{6,22},{7,23},{8,24},{9,... | collective-permute-start | bytes 1536008 | tf_op jit(solution)/shard_map/ppermute | solution.py:96
  49.2 13.0 %collective-permute-start.8 = (bf16[40,6400]{1,0:T(8,128)(2,1)S(1)}, bf16[40,6400]{1,0:T(8,128)(2,1)S(1)}, u32[]{:S(2)}, u32[]{:S(2)}) collective-permute-start(bf16[40,6400]{1,0:T(8,128)(2,1)S(1)} %select_select_fusion), channel_id=1, source_target_pairs={{0,8},{1,9},{2,10},{3,11},{4,12},{5,13},{6,14},{7,15},{8,0},{9,1},... | collective-permute-start | bytes 1536008 | tf_op jit(solution)/shard_map/ppermute | solution.py:96
  50.4 11.8 %collective-permute-start.7 = (bf16[40,6400]{1,0:T(8,128)(2,1)S(1)}, bf16[40,6400]{1,0:T(8,128)(2,1)S(1)}, u32[]{:S(2)}, u32[]{:S(2)}) collective-permute-start(bf16[40,6400]{1,0:T(8,128)(2,1)S(1)} %select_select_fusion), channel_id=1, source_target_pairs={{1,2},{2,1},{5,6},{6,5},{9,10},{10,9},{13,14},{14,13},{17,18},{18,... | collective-permute-start | bytes 1536008 | tf_op jit(solution)/shard_map/ppermute | solution.py:96
  51.1 12.7 %collective-permute-start.6 = (bf16[40,6400]{1,0:T(8,128)(2,1)S(1)}, bf16[40,6400]{1,0:T(8,128)(2,1)S(1)}, u32[]{:S(2)}, u32[]{:S(2)}) collective-permute-start(bf16[40,6400]{1,0:T(8,128)(2,1)S(1)} %select_select_fusion), channel_id=1, source_target_pairs={{0,1},{1,0},{2,3},{3,2},{4,5},{5,4},{6,7},{7,6},{8,9},{9,8},{10,11... | collective-permute-start | bytes 1536008 | tf_op jit(solution)/shard_map/ppermute | solution.py:96
  55.6 26.2 %copy-start.18 = (bf16[40,6400]{1,0:T(8,128)(2,1)S(1)}, bf16[40,6400]{1,0:T(8,128)(2,1)}, u32[]{:S(2)}) copy-start(bf16[40,6400]{1,0:T(8,128)(2,1)} %get-tuple-element.120) | copy-start | bytes 1536004
  61.2 15.3 %copy-start.6 = (bf16[40,6400]{1,0:T(8,128)(2,1)}, bf16[40,6400]{1,0:T(8,128)(2,1)S(1)}, u32[]{:S(2)}) copy-start(bf16[40,6400]{1,0:T(8,128)(2,1)S(1)} %collective-permute-done.9) | copy-start | bytes 1536004
  63.8 15.5 %collective-permute-start.13 = (bf16[40,6400]{1,0:T(8,128)(2,1)S(1)}, bf16[40,6400]{1,0:T(8,128)(2,1)S(1)}, u32[]{:S(2)}, u32[]{:S(2)}) collective-permute-start(bf16[40,6400]{1,0:T(8,128)(2,1)S(1)} %collective-permute-done.6), channel_id=1, source_target_pairs={{1,2},{2,1},{5,6},{6,5},{9,10},{10,9},{13,14},{14,13},{17,18},{18,... | collective-permute-start | bytes 1536008 | tf_op jit(solution)/shard_map/ppermute | solution.py:96
  64.5 11.8 %collective-permute-start.12 = (bf16[40,6400]{1,0:T(8,128)(2,1)S(1)}, bf16[40,6400]{1,0:T(8,128)(2,1)S(1)}, u32[]{:S(2)}, u32[]{:S(2)}) collective-permute-start(bf16[40,6400]{1,0:T(8,128)(2,1)S(1)} %collective-permute-done.6), channel_id=1, source_target_pairs={{0,16},{1,17},{2,18},{3,19},{4,20},{5,21},{6,22},{7,23},{8,24},{9,... | collective-permute-start | bytes 1536008 | tf_op jit(solution)/shard_map/ppermute | solution.py:96
  64.8 11.5 %collective-permute-start.11 = (bf16[40,6400]{1,0:T(8,128)(2,1)S(1)}, bf16[40,6400]{1,0:T(8,128)(2,1)S(1)}, u32[]{:S(2)}, u32[]{:S(2)}) collective-permute-start(bf16[40,6400]{1,0:T(8,128)(2,1)S(1)} %collective-permute-done.6), channel_id=1, source_target_pairs={{0,8},{1,9},{2,10},{3,11},{4,12},{5,13},{6,14},{7,15},{8,0},{9,1},... | collective-permute-start | bytes 1536008 | tf_op jit(solution)/shard_map/ppermute | solution.py:96
  65.0 14.3 %collective-permute-start.14 = (bf16[40,6400]{1,0:T(8,128)(2,1)S(1)}, bf16[40,6400]{1,0:T(8,128)(2,1)S(1)}, u32[]{:S(2)}, u32[]{:S(2)}) collective-permute-start(bf16[40,6400]{1,0:T(8,128)(2,1)S(1)} %collective-permute-done.7), channel_id=1, source_target_pairs={{1,0},{2,3},{5,4},{6,7},{9,8},{10,11},{13,12},{14,15},{17,16},{18,... | collective-permute-start | bytes 1536008 | tf_op jit(solution)/shard_map/ppermute | solution.py:96
  76.3 17.2 %copy-start.8 = (bf16[40,6400]{1,0:T(8,128)(2,1)}, bf16[40,6400]{1,0:T(8,128)(2,1)S(1)}, u32[]{:S(2)}) copy-start(bf16[40,6400]{1,0:T(8,128)(2,1)S(1)} %collective-permute-done.12) | copy-start | bytes 1536004
  76.3 17.1 %copy-start.9 = (bf16[40,6400]{1,0:T(8,128)(2,1)}, bf16[40,6400]{1,0:T(8,128)(2,1)S(1)}, u32[]{:S(2)}) copy-start(bf16[40,6400]{1,0:T(8,128)(2,1)S(1)} %collective-permute-done.11) | copy-start | bytes 1536004
  79.3 25.3 %collective-permute-start.16 = (bf16[2,40,3200]{2,1,0:T(8,128)(2,1)S(1)}, bf16[2,40,3200]{2,1,0:T(8,128)(2,1)S(1)}, u32[]{:S(2)}, u32[]{:S(2)}) collective-permute-start(bf16[2,40,3200]{2,1,0:T(8,128)(2,1)S(1)} %pad_maximum_fusion.2), channel_id=1, source_target_pairs={{0,16},{1,17},{2,18},{3,19},{4,20},{5,21},{6,22},{7,23},{8,24},{9,... | collective-permute-start | bytes 1536008 | tf_op jit(solution)/shard_map/ppermute | solution.py:96
  80.5 24.1 %collective-permute-start.17 = (bf16[2,40,3200]{2,1,0:T(8,128)(2,1)S(1)}, bf16[2,40,3200]{2,1,0:T(8,128)(2,1)S(1)}, u32[]{:S(2)}, u32[]{:S(2)}) collective-permute-start(bf16[2,40,3200]{2,1,0:T(8,128)(2,1)S(1)} %pad_maximum_fusion.3), channel_id=1, source_target_pairs={{0,8},{1,9},{2,10},{3,11},{4,12},{5,13},{6,14},{7,15},{8,0},{9,1},... | collective-permute-start | bytes 1536008 | tf_op jit(solution)/shard_map/ppermute | solution.py:96
  81.8 38.9 %collective-permute-start.18 = (bf16[40,6400]{1,0:T(8,128)(2,1)S(1)}, bf16[40,6400]{1,0:T(8,128)(2,1)S(1)}, u32[]{:S(2)}, u32[]{:S(2)}) collective-permute-start(bf16[40,6400]{1,0:T(8,128)(2,1)S(1)} %copy-done.18), channel_id=1, source_target_pairs={{3,0},{0,1},{5,2},{6,3},{1,4},{2,5},{7,6},{4,7},{11,8},{8,9},{13,1... | collective-permute-start | bytes 1536008 | tf_op jit(solution)/shard_map/ppermute | solution.py:96
  83.3 21.1 %collective-permute-start.15 = (bf16[40,6400]{1,0:T(8,128)(2,1)S(1)}, bf16[40,6400]{1,0:T(8,128)(2,1)S(1)}, u32[]{:S(2)}, u32[]{:S(2)}) collective-permute-start(bf16[40,6400]{1,0:T(8,128)(2,1)S(1)} %collective-permute-done.13), channel_id=1, source_target_pairs={{1,0},{2,3},{5,4},{6,7},{9,8},{10,11},{13,12},{14,15},{17,16},{18,... | collective-permute-start | bytes 1536008 | tf_op jit(solution)/shard_map/ppermute | solution.py:96
  84.6 57.1 %collective-permute-start.26 = (bf16[40,25600]{1,0:T(8,128)(2,1)}, bf16[40,25600]{1,0:T(8,128)(2,1)}, u32[]{:S(2)}, u32[]{:S(2)}) collective-permute-start(bf16[40,25600]{1,0:T(8,128)(2,1)} %pick.3.refs_0_), channel_id=1, source_target_pairs={{4,2},{5,3},{2,4},{3,5},{12,10},{13,11},{10,12},{11,13},{20,18},{2... | collective-permute-start | bytes 6144008 | tf_op jit(solution)/shard_map/ppermute | solution.py:96
  104.6 16.1 %copy-start = (bf16[2,40,6400]{2,1,0:T(8,128)(2,1)}, bf16[2,40,6400]{2,1,0:T(8,128)(2,1)S(1)}, u32[]{:S(2)}) copy-start(bf16[2,40,6400]{2,1,0:T(8,128)(2,1)S(1)} %pad_maximum_fusion.refs_6_.refs_10_.refs_2_.refs_7_) | copy-start | bytes 3072004
  104.6 20.0 %collective-permute-start.20 = (bf16[2,40,6400]{2,1,0:T(8,128)(2,1)S(1)}, bf16[2,40,6400]{2,1,0:T(8,128)(2,1)S(1)}, u32[]{:S(2)}, u32[]{:S(2)}) collective-permute-start(bf16[2,40,6400]{2,1,0:T(8,128)(2,1)S(1)} %pad_maximum_fusion.refs_6_.refs_10_.refs_2_.refs_7_), channel_id=1, source_target_pairs={{0,16},{1,17},{2,18},{3,19},{4,20},{5,21},{6,22},{7,23},{8,24},{9,... | collective-permute-start | bytes 3072008 | tf_op jit(solution)/shard_map/ppermute | solution.py:96
  104.9 25.7 %collective-permute-start.19 = (bf16[2,40,6400]{2,1,0:T(8,128)(2,1)S(1)}, bf16[2,40,6400]{2,1,0:T(8,128)(2,1)S(1)}, u32[]{:S(2)}, u32[]{:S(2)}) collective-permute-start(bf16[2,40,6400]{2,1,0:T(8,128)(2,1)S(1)} %pad_maximum_fusion.refs_6_.refs_10_.refs_2_.refs_7_), channel_id=1, source_target_pairs={{0,8},{1,9},{2,10},{3,11},{4,12},{5,13},{6,14},{7,15},{8,0},{9,1},... | collective-permute-start | bytes 3072008 | tf_op jit(solution)/shard_map/ppermute | solution.py:96
  106.5 25.0 %collective-permute-start.22 = (bf16[40,16000]{1,0:T(8,128)(2,1)}, bf16[40,16000]{1,0:T(8,128)(2,1)}, u32[]{:S(2)}, u32[]{:S(2)}) collective-permute-start(bf16[40,16000]{1,0:T(8,128)(2,1)} %collective-permute-done.5.refs_1_.refs_4_), channel_id=1, source_target_pairs={{0,4},{1,5},{2,6},{3,7},{4,0},{5,1},{6,2},{7,3},{8,12},{9,13},{10,... | collective-permute-start | bytes 3840008 | tf_op jit(solution)/shard_map/ppermute | solution.py:96
  120.7 10.8 %collective-permute-start.23 = (bf16[40,6400]{1,0:T(8,128)(2,1)S(1)}, bf16[40,6400]{1,0:T(8,128)(2,1)S(1)}, u32[]{:S(2)}, u32[]{:S(2)}) collective-permute-start(bf16[40,6400]{1,0:T(8,128)(2,1)S(1)} %collective-permute-done.18.refs_2_.refs_5_), channel_id=1, source_target_pairs={{0,4},{1,5},{2,6},{3,7},{4,0},{5,1},{6,2},{7,3},{8,12},{9,13},{10,... | collective-permute-start | bytes 1536008 | tf_op jit(solution)/shard_map/ppermute | solution.py:96
  124.6 17.0 %copy-start.1 = (bf16[2,40,6400]{2,1,0:T(8,128)(2,1)}, bf16[2,40,6400]{2,1,0:T(8,128)(2,1)S(1)}, u32[]{:S(2)}) copy-start(bf16[2,40,6400]{2,1,0:T(8,128)(2,1)S(1)} %collective-permute-done.20.refs_8_.refs_12_.refs_4_.refs_9_) | copy-start | bytes 3072004
  124.6 6.8 %collective-permute-start.21 = (bf16[40,3200]{1,0:T(8,128)(2,1)}, bf16[40,3200]{1,0:T(8,128)(2,1)S(1)}, u32[]{:S(2)}, u32[]{:S(2)}) collective-permute-start(bf16[40,3200]{1,0:T(8,128)(2,1)} %collective-permute-done.1.refs_0_.refs_3_), channel_id=1, source_target_pairs={{0,4},{1,5},{2,6},{3,7},{4,0},{5,1},{6,2},{7,3},{8,12},{9,13},{10,... | collective-permute-start | bytes 768008 | tf_op jit(solution)/shard_map/ppermute | solution.py:96
  132.2 13.5 %collective-permute-start.24 = (bf16[2,40,3200]{2,1,0:T(8,128)(2,1)}, bf16[2,40,3200]{2,1,0:T(8,128)(2,1)S(1)}, u32[]{:S(2)}, u32[]{:S(2)}) collective-permute-start(bf16[2,40,3200]{2,1,0:T(8,128)(2,1)} %slice.42), channel_id=1, source_target_pairs={{0,16},{1,17},{2,18},{3,19},{4,20},{5,21},{6,22},{7,23},{8,24},{9,... | collective-permute-start | bytes 1536008 | tf_op jit(solution)/shard_map/ppermute | solution.py:96
  132.4 13.2 %collective-permute-start.25 = (bf16[2,40,3200]{2,1,0:T(8,128)(2,1)}, bf16[2,40,3200]{2,1,0:T(8,128)(2,1)S(1)}, u32[]{:S(2)}, u32[]{:S(2)}) collective-permute-start(bf16[2,40,3200]{2,1,0:T(8,128)(2,1)} %slice.43), channel_id=1, source_target_pairs={{0,8},{1,9},{2,10},{3,11},{4,12},{5,13},{6,14},{7,15},{8,0},{9,1},... | collective-permute-start | bytes 1536008 | tf_op jit(solution)/shard_map/ppermute | solution.py:96
  145.7 9.4 %collective-permute-start.27 = (bf16[40,25600]{1,0:T(8,128)(2,1)}, bf16[40,25600]{1,0:T(8,128)(2,1)}, u32[]{:S(2)}, u32[]{:S(2)}) collective-permute-start(bf16[40,25600]{1,0:T(8,128)(2,1)} %collective-permute-done.26.refs_4_), channel_id=1, source_target_pairs={{0,4},{1,5},{2,6},{3,7},{4,0},{5,1},{6,2},{7,3},{8,12},{9,13},{10,... | collective-permute-start | bytes 6144008 | tf_op jit(solution)/shard_map/ppermute | solution.py:96
  185.1 2.9 %collective-permute-start.28 = (bf16[40,10240]{1,0:T(8,128)(2,1)}, bf16[40,10240]{1,0:T(8,128)(2,1)S(1)}, u32[]{:S(2)}, u32[]{:S(2)}) collective-permute-start(bf16[40,10240]{1,0:T(8,128)(2,1)} %get-tuple-element.135), channel_id=1, source_target_pairs={{0,4},{1,5},{2,6},{3,7},{4,0},{5,1},{6,2},{7,3},{8,12},{9,13},{10,... | collective-permute-start | bytes 2457608 | tf_op jit(solution)/shard_map/ppermute | solution.py:96
  185.9 16.5 %collective-permute-start.30 = (bf16[40,15360]{1,0:T(8,128)(2,1)}, bf16[40,15360]{1,0:T(8,128)(2,1)S(1)}, u32[]{:S(2)}, u32[]{:S(2)}) collective-permute-start(bf16[40,15360]{1,0:T(8,128)(2,1)} %get-tuple-element.137), channel_id=1, source_target_pairs={{0,4},{1,5},{2,6},{3,7},{4,0},{5,1},{6,2},{7,3},{8,12},{9,13},{10,... | collective-permute-start | bytes 3686408 | tf_op jit(solution)/shard_map/ppermute | solution.py:96
  190.3 21.7 %collective-permute-start.29 = (bf16[40,10240]{1,0:T(8,128)(2,1)}, bf16[40,10240]{1,0:T(8,128)(2,1)}, u32[]{:S(2)}, u32[]{:S(2)}) collective-permute-start(bf16[40,10240]{1,0:T(8,128)(2,1)} %add_convert_fusion.1), channel_id=1, source_target_pairs={{0,3},{1,0},{2,5},{3,6},{4,1},{5,2},{6,7},{7,4},{8,11},{9,8},{10,1... | collective-permute-start | bytes 2457608 | tf_op jit(solution)/shard_map/ppermute | solution.py:96
  197.7 21.6 %collective-permute-start.34 = (bf16[40,6400]{1,0:T(8,128)(2,1)}, bf16[40,6400]{1,0:T(8,128)(2,1)}, u32[]{:S(2)}, u32[]{:S(2)}) collective-permute-start(bf16[40,6400]{1,0:T(8,128)(2,1)} %get-tuple-element.147), channel_id=1, source_target_pairs={{0,4},{1,5},{2,6},{3,7},{4,0},{5,1},{6,2},{7,3},{8,12},{9,13},{10,... | collective-permute-start | bytes 1536008 | tf_op jit(solution)/shard_map/ppermute | solution.py:96
  201.8 22.0 %collective-permute-start.36 = (bf16[40,6400]{1,0:T(8,128)(2,1)}, bf16[40,6400]{1,0:T(8,128)(2,1)}, u32[]{:S(2)}, u32[]{:S(2)}) collective-permute-start(bf16[40,6400]{1,0:T(8,128)(2,1)} %get-tuple-element.149), channel_id=1, source_target_pairs={{0,4},{1,5},{2,6},{3,7},{4,0},{5,1},{6,2},{7,3},{8,12},{9,13},{10,... | collective-permute-start | bytes 1536008 | tf_op jit(solution)/shard_map/ppermute | solution.py:96
  201.9 28.2 %collective-permute-start.38 = (bf16[40,6400]{1,0:T(8,128)(2,1)}, bf16[40,6400]{1,0:T(8,128)(2,1)}, u32[]{:S(2)}, u32[]{:S(2)}) collective-permute-start(bf16[40,6400]{1,0:T(8,128)(2,1)} %get-tuple-element.151), channel_id=1, source_target_pairs={{0,4},{1,5},{2,6},{3,7},{4,0},{5,1},{6,2},{7,3},{8,12},{9,13},{10,... | collective-permute-start | bytes 1536008 | tf_op jit(solution)/shard_map/ppermute | solution.py:96
  202.4 32.0 %collective-permute-start.32 = (bf16[40,6400]{1,0:T(8,128)(2,1)}, bf16[40,6400]{1,0:T(8,128)(2,1)}, u32[]{:S(2)}, u32[]{:S(2)}) collective-permute-start(bf16[40,6400]{1,0:T(8,128)(2,1)} %get-tuple-element.142), channel_id=1, source_target_pairs={{0,4},{1,5},{2,6},{3,7},{4,0},{5,1},{6,2},{7,3},{8,12},{9,13},{10,... | collective-permute-start | bytes 1536008 | tf_op jit(solution)/shard_map/ppermute | solution.py:96
  212.0 30.6 %collective-permute-start.31 = (bf16[40,15360]{1,0:T(8,128)(2,1)S(1)}, bf16[40,15360]{1,0:T(8,128)(2,1)}, u32[]{:S(2)}, u32[]{:S(2)}) collective-permute-start(bf16[40,15360]{1,0:T(8,128)(2,1)S(1)} %add_convert_fusion), channel_id=1, source_target_pairs={{0,3},{1,0},{2,5},{3,6},{4,1},{5,2},{6,7},{7,4},{8,11},{9,8},{10,1... | collective-permute-start | bytes 3686408 | tf_op jit(solution)/shard_map/ppermute | solution.py:96
  221.6 46.0 %collective-permute-start.35 = (bf16[40,6400]{1,0:T(8,128)(2,1)}, bf16[40,6400]{1,0:T(8,128)(2,1)}, u32[]{:S(2)}, u32[]{:S(2)}) collective-permute-start(bf16[40,6400]{1,0:T(8,128)(2,1)} %add_convert_fusion.4.refs_2_), channel_id=1, source_target_pairs={{2,4},{3,5},{4,2},{5,3},{10,12},{11,13},{12,10},{13,11},{18,20},{1... | collective-permute-start | bytes 1536008 | tf_op jit(solution)/shard_map/ppermute | solution.py:96
  225.9 47.1 %collective-permute-start.37 = (bf16[40,6400]{1,0:T(8,128)(2,1)}, bf16[40,6400]{1,0:T(8,128)(2,1)}, u32[]{:S(2)}, u32[]{:S(2)}) collective-permute-start(bf16[40,6400]{1,0:T(8,128)(2,1)} %add_convert_fusion.3.refs_3_), channel_id=1, source_target_pairs={{2,4},{3,5},{4,2},{5,3},{10,12},{11,13},{12,10},{13,11},{18,20},{1... | collective-permute-start | bytes 1536008 | tf_op jit(solution)/shard_map/ppermute | solution.py:96
  232.1 46.4 %collective-permute-start.39 = (bf16[40,6400]{1,0:T(8,128)(2,1)}, bf16[40,6400]{1,0:T(8,128)(2,1)}, u32[]{:S(2)}, u32[]{:S(2)}) collective-permute-start(bf16[40,6400]{1,0:T(8,128)(2,1)} %add_convert_fusion.2.refs_4_), channel_id=1, source_target_pairs={{2,4},{3,5},{4,2},{5,3},{10,12},{11,13},{12,10},{13,11},{18,20},{1... | collective-permute-start | bytes 1536008 | tf_op jit(solution)/shard_map/ppermute | solution.py:96
  236.4 47.6 %collective-permute-start.33 = (bf16[40,6400]{1,0:T(8,128)(2,1)}, bf16[40,6400]{1,0:T(8,128)(2,1)}, u32[]{:S(2)}, u32[]{:S(2)}) collective-permute-start(bf16[40,6400]{1,0:T(8,128)(2,1)} %add_convert_fusion.5.refs_1_), channel_id=1, source_target_pairs={{2,4},{3,5},{4,2},{5,3},{10,12},{11,13},{12,10},{13,11},{18,20},{1... | collective-permute-start | bytes 1536008 | tf_op jit(solution)/shard_map/ppermute | solution.py:96
  (11 other events, 93.4 us)
